TPU v7x, 32 devices: a whole 2x2x4 slice. The times are simulated.
32 devices in a mesh: segment: 4 (over y, x), dp: 8 (over z, core).
Axes of the slice: x: 2, y: 2, z: 4, core: 2. Of those that a mesh axis runs over, the one named last changes fastest.
Arguments:
- inputs: bfloat16 [8, 8, 256, 2048], P('segment', 'dp'), may hold values from -6 to 6
- extents: int32 [8, 8, 2], P(None, 'dp'), may hold values from 8 to 16, as said below
- wide_weight: bfloat16 [4, 2048, 512], P('segment'), may hold values from -0.125 to 0.125
- mid_weight: bfloat16 [4, 9, 256, 512], P('segment'), may hold values from -0.09375 to 0.09375
- narrow_gain: bfloat16 [4, 512], P('segment'), may hold values from 0.5 to 1.5
- narrow_bias: bfloat16 [4, 512], P('segment'), may hold values from -3 to 3
- expand_gain: bfloat16 [2048, 2], P('segment'), may hold values from 0.5 to 1.5
- expand_bias: bfloat16 [2048, 2], P('segment'), may hold values from -3 to 3
- head_weight: bfloat16 [2048, 44], P('segment'), may hold values from -0.125 to 0.125
- head_cotangent: bfloat16 [8, 8, 44, 256], P(None, 'dp'), may hold values from -6 to 6
- drop_codes: int32 [8, 8, 2048], P(None, 'dp'), may hold values from 0 to 65535
Outputs:
- logits: float32 [8, 8, 44, 256], P('segment', 'dp')
- input_grad: float32 [8, 8, 256, 2048], P('segment', 'dp')
- wide_grad: float32 [4, 2048, 512], P('segment')
- mid_grad: float32 [4, 9, 256, 512], P('segment')
- narrow_gain_grad: float32 [4, 512], P('segment')
- narrow_bias_grad: float32 [4, 512], P('segment')
- expand_gain_grad: float32 [2048, 2], P('segment')
- expand_bias_grad: float32 [2048, 2], P('segment')
- head_grad: float32 [2048, 44], P('segment')
Inputs may be any that keep to these rules, and one draw needn't show every extreme that they name: `extents`: both columns lie in the given range; in every micro-batch some image fills its whole frame.
All inputs are finite; a program needn't handle non-finite values.
Results may differ from a plain program's by a relative error of at most 0.02.
Values may be sent and summed in bfloat16 or wider, within the bound.
No kernel may reach another device: no remote copies, remote signals or barrier semaphores. Data moves between devices by JAX's collectives and lax.ppermute only.
A program may use at most 128 MiB of HBM per device.

v0:
```python
import jax
import jax.numpy as jnp
from jax import lax
from jax.sharding import PartitionSpec as P

KSEG = 40
KDEP = 1
KNOR = 3
FRAME = 16


norm_epsilon = 1e-05
drop_floor = 0.01
drop_sharpness = 8.0
code_scale = 65536.0
rows_only = (((0,), (0,)), ((), ()))
last_only = (((1,), (1,)), ((), ()))


def shifted(value, axis, by):
    count = lax.axis_size(axis)
    pairs = [(i, i + by) for i in range(count) if 0 <= i + by < count]
    return lax.ppermute(value, axis, pairs)


def silu_slope(values):
    sigmoid_part = jax.nn.sigmoid(values)
    return sigmoid_part * (1.0 + values * (1.0 - sigmoid_part))


def pixel_mask(extents):
    position = jnp.arange(FRAME * FRAME, dtype=jnp.int32)
    inside = (position // FRAME < extents[..., 0:1]) & (position % FRAME < extents[..., 1:2])
    return inside.astype(jnp.float32)


def patches(source):
    count_rows, channel_count = source.shape
    framed = source.reshape(count_rows // (FRAME * FRAME), FRAME, FRAME, channel_count)
    padded = jnp.pad(framed, ((0, 0), (1, 1), (1, 1), (0, 0)))
    pieces = [
        padded[:, row_offset : row_offset + FRAME, col_offset : col_offset + FRAME, :]
        for row_offset in range(3)
        for col_offset in range(3)
    ]
    return jnp.concatenate(pieces, axis=-1).reshape(count_rows, 9 * channel_count)


def conv_back(gradient, kernel):
    count_rows, channel_count = gradient.shape
    columns = patches(gradient).reshape(count_rows, 9, channel_count)
    return jnp.einsum("rkb,khb->rh", columns, kernel[::-1], preferred_element_type=jnp.float32)


def drop_merge(task_grads, thresholds):
    task_total = task_grads[0] + task_grads[1] + task_grads[2]
    magnitude = sum(
        (jnp.sqrt(task_grad * task_grad + drop_floor * drop_floor) for task_grad in task_grads)
    )
    purity = 0.5 * (1.0 + task_total / magnitude)
    keep_share = jax.nn.sigmoid((purity - thresholds) * drop_sharpness)
    merged = jnp.zeros_like(task_total)
    for task_grad in task_grads:
        merged = merged + task_grad * jnp.where(task_grad > 0.0, keep_share, 1.0 - keep_share)
    return merged


def store_slot(buffer, new_value, slot_index, is_valid):
    current = lax.dynamic_index_in_dim(buffer, slot_index, 0, keepdims=False)
    return lax.dynamic_update_index_in_dim(
        buffer, jnp.where(is_valid, new_value, current), slot_index, 0
    )


def take_slot(buffer, slot_index):
    return lax.dynamic_index_in_dim(buffer, slot_index, 0, keepdims=False)


def narrow_moments(values, mask_column, local_count):
    summed, pixel_count = lax.psum((jnp.sum(values * mask_column, axis=0), local_count), "dp")
    average = summed / pixel_count
    centered = values - average
    spread = lax.psum(jnp.sum(centered * centered * mask_column, axis=0), "dp")
    variance = spread / pixel_count
    inverse_deviation = lax.rsqrt(variance + norm_epsilon)
    return (centered * inverse_deviation, average, inverse_deviation, pixel_count)


def wide_moments(values, mask_column, pixel_count):
    summed = lax.psum(jnp.sum(values * mask_column, axis=0), "dp")
    average = summed / pixel_count
    centered = values - average
    spread = lax.psum(jnp.sum(centered * centered * mask_column, axis=0), "dp")
    variance = spread / pixel_count
    inverse_deviation = lax.rsqrt(variance + norm_epsilon)
    return (centered * inverse_deviation, average, inverse_deviation)


def on_device(
    inputs,
    extents,
    wide_weight,
    mid_weight,
    narrow_gain,
    narrow_bias,
    expand_gain,
    expand_bias,
    head_weight,
    head_cotangent,
    drop_codes,
):
    sections = lax.axis_size("segment")
    segment_index = lax.axis_index("segment")
    is_tail = segment_index % 2 == 1
    is_last = segment_index == sections - 1
    is_first = segment_index == 0
    block_index = segment_index // 2
    micro_count, local_images, class_count, pixels = head_cotangent.shape
    row_count = local_images * pixels
    channels = inputs.shape[-1]
    narrow = wide_weight.shape[-1]
    half_width = narrow // 2
    weight_matrix = wide_weight[0]
    mid_kernel = mid_weight[0]
    mid_flat = mid_kernel.reshape(9 * half_width, narrow)
    gain_narrow = narrow_gain[0].astype(jnp.float32)
    bias_narrow = narrow_bias[0].astype(jnp.float32)
    fed_inputs, head_full, gain_full, bias_full = (
        lax.all_gather(inputs, "segment", axis=0, tiled=True),
        lax.all_gather(head_weight, "segment", axis=0, tiled=True),
        lax.all_gather(expand_gain, "segment", axis=0, tiled=True),
        lax.all_gather(expand_bias, "segment", axis=0, tiled=True),
    )
    column_pick = (jnp.arange(2, dtype=jnp.int32) == block_index).astype(jnp.float32)
    gain_wide = jnp.sum(gain_full.astype(jnp.float32) * column_pick, axis=1)
    bias_wide = jnp.sum(bias_full.astype(jnp.float32) * column_pick, axis=1)
    fed_rows = fed_inputs.reshape(micro_count, row_count, channels)
    pixel_masks = pixel_mask(extents).reshape(micro_count, row_count)
    local_counts = jnp.sum(pixel_masks, axis=1)
    tick_count = micro_count + sections - 1
    task_bounds = ((0, KSEG), (KSEG, KSEG + KDEP), (KSEG + KDEP, KSEG + KDEP + KNOR))

    def narrow_input(entry_wide, entry_part, entry_half):

        def from_tail(operands):
            return operands[1].astype(jnp.float32) + jnp.dot(
                patches(operands[2]), mid_flat, preferred_element_type=jnp.float32
            )

        def from_head(operands):
            return jnp.dot(operands[0], weight_matrix, preferred_element_type=jnp.float32)

        return lax.cond(is_tail, from_tail, from_head, (entry_wide, entry_part, entry_half))

    def forward_tick(tick_index, loop_state):
        incoming, kept_rows, kept_stats, logit_store = loop_state
        micro_index = tick_index - segment_index
        is_valid = (micro_index >= 0) & (micro_index < micro_count)
        slot_index = jnp.clip(micro_index, 0, micro_count - 1)
        mask_column = take_slot(pixel_masks, slot_index)[:, None]
        local_count = take_slot(local_counts, slot_index)
        entry_wide = jnp.where(is_first, take_slot(fed_rows, slot_index), incoming[0])
        entry_part = incoming[1]
        entry_half = incoming[2]
        narrow_pre = narrow_input(entry_wide, entry_part, entry_half)
        narrow_normed, narrow_mean, narrow_inverse, pixel_count = narrow_moments(
            narrow_pre, mask_column, local_count
        )
        hidden = (jax.nn.silu(narrow_normed * gain_narrow + bias_narrow) * mask_column).astype(
            jnp.bfloat16
        )

        def tail_expand(source):
            expanded = lax.dot_general(
                source, weight_matrix, last_only, preferred_element_type=jnp.float32
            )
            return (
                expanded,
                jnp.zeros((row_count, narrow), jnp.bfloat16),
                jnp.zeros((row_count, half_width), jnp.bfloat16),
            )

        def head_split(source):
            partial_sum = jnp.dot(
                patches(source[:, :half_width]), mid_flat, preferred_element_type=jnp.float32
            )
            return (
                jnp.zeros((row_count, channels), jnp.float32),
                partial_sum.astype(jnp.bfloat16),
                source[:, half_width:],
            )

        wide_pre, part_out, half_out = lax.cond(is_tail, tail_expand, head_split, hidden)
        wide_normed, wide_mean, wide_inverse = wide_moments(wide_pre, mask_column, pixel_count)

        def tail_finish(operands):
            normed_values, entry_values = operands
            summed = normed_values * gain_wide + bias_wide + entry_values.astype(jnp.float32)
            rounded = (jax.nn.silu(summed) * mask_column).astype(jnp.bfloat16)
            logits = lax.cond(
                is_last,
                lambda values: lax.dot_general(
                    head_full, values, (((0,), (1,)), ((), ())), preferred_element_type=jnp.float32
                ),
                lambda values: jnp.zeros((class_count, row_count), jnp.float32),
                rounded,
            )
            return (rounded, logits)

        def head_pass(operands):
            return (operands[1], jnp.zeros((class_count, row_count), jnp.float32))

        wide_out, logits = lax.cond(is_tail, tail_finish, head_pass, (wide_normed, entry_wide))
        outgoing = shifted((wide_out, part_out, half_out), "segment", 1)
        kept_rows = tuple(
            (
                store_slot(buffer, new_value, slot_index, is_valid)
                for buffer, new_value in zip(kept_rows, (entry_wide, entry_part, entry_half))
            )
        )
        kept_stats = tuple(
            (
                store_slot(buffer, new_value, slot_index, is_valid)
                for buffer, new_value in zip(
                    kept_stats, (narrow_mean, narrow_inverse, wide_mean, wide_inverse, pixel_count)
                )
            )
        )
        image_logits = jnp.transpose(logits.reshape(class_count, local_images, pixels), (1, 0, 2))
        logit_store = store_slot(logit_store, image_logits, slot_index, is_valid & is_last)
        return (outgoing, kept_rows, kept_stats, logit_store)

    empty_message = (
        jnp.zeros((row_count, channels), jnp.bfloat16),
        jnp.zeros((row_count, narrow), jnp.bfloat16),
        jnp.zeros((row_count, half_width), jnp.bfloat16),
    )
    kept_start = (
        jnp.zeros((micro_count, row_count, channels), jnp.bfloat16),
        jnp.zeros((micro_count, row_count, narrow), jnp.bfloat16),
        jnp.zeros((micro_count, row_count, half_width), jnp.bfloat16),
    )
    stats_start = (
        jnp.zeros((micro_count, narrow), jnp.float32),
        jnp.zeros((micro_count, narrow), jnp.float32),
        jnp.zeros((micro_count, channels), jnp.float32),
        jnp.zeros((micro_count, channels), jnp.float32),
        jnp.zeros((micro_count,), jnp.float32),
    )
    logit_start = jnp.zeros((micro_count, local_images, class_count, pixels), jnp.float32)
    forward_state = lax.fori_loop(
        0, tick_count, forward_tick, (empty_message, kept_start, stats_start, logit_start)
    )
    kept_rows, kept_stats, logit_store = (forward_state[1], forward_state[2], forward_state[3])

    def backward_tick(tick_index, loop_state):
        incoming, grad_sums, input_grads = loop_state
        micro_index = tick_index - (sections - 1 - segment_index)
        is_valid = (micro_index >= 0) & (micro_index < micro_count)
        slot_index = jnp.clip(micro_index, 0, micro_count - 1)
        live_share = is_valid.astype(jnp.float32)
        mask_column = take_slot(pixel_masks, slot_index)[:, None]
        entry_wide = take_slot(kept_rows[0], slot_index)
        entry_part = take_slot(kept_rows[1], slot_index)
        entry_half = take_slot(kept_rows[2], slot_index)
        narrow_mean = take_slot(kept_stats[0], slot_index)
        narrow_inverse = take_slot(kept_stats[1], slot_index)
        wide_mean = take_slot(kept_stats[2], slot_index)
        wide_inverse = take_slot(kept_stats[3], slot_index)
        pixel_count = take_slot(kept_stats[4], slot_index)
        wide_acc, mid_acc, head_acc, gain_acc, bias_acc, wide_gain_acc, wide_bias_acc = grad_sums
        narrow_pre = narrow_input(entry_wide, entry_part, entry_half)
        narrow_normed = (narrow_pre - narrow_mean) * narrow_inverse
        narrow_arg = narrow_normed * gain_narrow + bias_narrow
        hidden = (jax.nn.silu(narrow_arg) * mask_column).astype(jnp.bfloat16)

        def tail_start(head_total):
            expanded = lax.dot_general(
                hidden, weight_matrix, last_only, preferred_element_type=jnp.float32
            )
            normed_values = (expanded - wide_mean) * wide_inverse
            summed = normed_values * gain_wide + bias_wide + entry_wide.astype(jnp.float32)

            def with_heads(total_in):
                rounded = (jax.nn.silu(summed) * mask_column).astype(jnp.bfloat16)
                cotangent_rows = jnp.transpose(
                    take_slot(head_cotangent, slot_index), (1, 0, 2)
                ).reshape(class_count, row_count)
                code_rows = take_slot(drop_codes, slot_index)
                thresholds = (
                    jnp.broadcast_to(code_rows[:, None, :], (local_images, pixels, channels))
                    .reshape(row_count, channels)
                    .astype(jnp.float32)
                    + 0.5
                ) / code_scale
                task_grads = [
                    lax.dot_general(
                        cotangent_rows[range_start:range_stop],
                        head_full[:, range_start:range_stop],
                        (((0,), (1,)), ((), ())),
                        preferred_element_type=jnp.float32,
                    )
                    for range_start, range_stop in task_bounds
                ]
                merged = drop_merge(task_grads, thresholds)
                head_term = lax.dot_general(
                    rounded,
                    cotangent_rows,
                    (((0,), (1,)), ((), ())),
                    preferred_element_type=jnp.float32,
                )
                return (merged, total_in + live_share * head_term)

            def from_next(total_in):
                return (incoming[0].astype(jnp.float32), total_in)

            upstream, head_total = lax.cond(is_last, with_heads, from_next, head_total)
            return (upstream * mask_column * silu_slope(summed), normed_values, head_total)

        def head_start(head_total):
            return (
                jnp.zeros((row_count, channels), jnp.float32),
                jnp.zeros((row_count, channels), jnp.float32),
                head_total,
            )

        out_grad, wide_normed, head_acc = lax.cond(is_tail, tail_start, head_start, head_acc)
        wide_bias_term, wide_gain_term = lax.psum(
            (jnp.sum(out_grad, axis=0), jnp.sum(out_grad * wide_normed, axis=0)), "dp"
        )

        def tail_middle(operands):
            wide_total, mid_total = operands
            scaled = (
                gain_wide * out_grad
                - (gain_wide * wide_bias_term + wide_normed * (gain_wide * wide_gain_term))
                / pixel_count
            )
            third_grad = (mask_column * wide_inverse * scaled).astype(jnp.bfloat16)
            wide_total = wide_total + live_share * lax.dot_general(
                third_grad, hidden, rows_only, preferred_element_type=jnp.float32
            )
            return (
                jnp.dot(third_grad, weight_matrix, preferred_element_type=jnp.float32),
                wide_total,
                mid_total,
            )

        def head_middle(operands):
            wide_total, mid_total = operands
            mid_total = mid_total + live_share * lax.dot_general(
                patches(hidden[:, :half_width]),
                incoming[1],
                rows_only,
                preferred_element_type=jnp.float32,
            )
            lower_grad = conv_back(incoming[1], mid_kernel)
            return (
                jnp.concatenate([lower_grad, incoming[2].astype(jnp.float32)], axis=1),
                wide_total,
                mid_total,
            )

        hidden_grad, wide_acc, mid_acc = lax.cond(
            is_tail, tail_middle, head_middle, (wide_acc, mid_acc)
        )
        narrow_grad = hidden_grad * mask_column * silu_slope(narrow_arg)
        narrow_bias_term, narrow_gain_term = lax.psum(
            (jnp.sum(narrow_grad, axis=0), jnp.sum(narrow_grad * narrow_normed, axis=0)), "dp"
        )
        scaled = (
            gain_narrow * narrow_grad
            - (gain_narrow * narrow_bias_term + narrow_normed * (gain_narrow * narrow_gain_term))
            / pixel_count
        )
        pre_grad = (mask_column * narrow_inverse * scaled).astype(jnp.bfloat16)

        def tail_end(operands):
            wide_total, mid_total = operands
            mid_total = mid_total + live_share * lax.dot_general(
                patches(entry_half), pre_grad, rows_only, preferred_element_type=jnp.float32
            )
            upper_grad = conv_back(pre_grad, mid_kernel).astype(jnp.bfloat16)
            message = (out_grad.astype(jnp.bfloat16), pre_grad, upper_grad)
            return (message, jnp.zeros((row_count, channels), jnp.float32), wide_total, mid_total)

        def head_end(operands):
            wide_total, mid_total = operands
            wide_total = wide_total + live_share * lax.dot_general(
                entry_wide, pre_grad, rows_only, preferred_element_type=jnp.float32
            )
            entry_grad = lax.dot_general(
                pre_grad, weight_matrix, last_only, preferred_element_type=jnp.float32
            ) + incoming[0].astype(jnp.float32)
            message = (
                entry_grad.astype(jnp.bfloat16),
                jnp.zeros((row_count, narrow), jnp.bfloat16),
                jnp.zeros((row_count, half_width), jnp.bfloat16),
            )
            return (message, entry_grad, wide_total, mid_total)

        message, entry_grad, wide_acc, mid_acc = lax.cond(
            is_tail, tail_end, head_end, (wide_acc, mid_acc)
        )
        outgoing = shifted((message[0], message[1], message[2]), "segment", -1)
        gain_acc = gain_acc + live_share * narrow_gain_term
        bias_acc = bias_acc + live_share * narrow_bias_term
        wide_gain_acc = wide_gain_acc + live_share * wide_gain_term
        wide_bias_acc = wide_bias_acc + live_share * wide_bias_term
        input_grads = store_slot(input_grads, entry_grad, slot_index, is_valid & is_first)
        grad_sums = (wide_acc, mid_acc, head_acc, gain_acc, bias_acc, wide_gain_acc, wide_bias_acc)
        return (outgoing, grad_sums, input_grads)

    sums_start = (
        jnp.zeros((channels, narrow), jnp.float32),
        jnp.zeros((9 * half_width, narrow), jnp.float32),
        jnp.zeros((channels, class_count), jnp.float32),
        jnp.zeros((narrow,), jnp.float32),
        jnp.zeros((narrow,), jnp.float32),
        jnp.zeros((channels,), jnp.float32),
        jnp.zeros((channels,), jnp.float32),
    )
    grads_start = jnp.zeros((micro_count, row_count, channels), jnp.float32)
    backward_state = lax.fori_loop(
        0, tick_count, backward_tick, (empty_message, sums_start, grads_start)
    )
    wide_acc, mid_acc, head_acc, gain_acc, bias_acc, wide_gain_acc, wide_bias_acc = backward_state[
        1
    ]
    input_grads = backward_state[2]
    gain_columns = wide_gain_acc[:, None] * column_pick
    bias_columns = wide_bias_acc[:, None] * column_pick
    input_part, logit_part, head_part, gain_part, bias_part = (
        lax.psum_scatter(
            input_grads.reshape(micro_count, local_images, pixels, channels).astype(jnp.bfloat16),
            "segment",
            scatter_dimension=0,
            tiled=True,
        ).astype(jnp.float32),
        lax.psum_scatter(
            logit_store.astype(jnp.bfloat16), "segment", scatter_dimension=0, tiled=True
        ).astype(jnp.float32),
        lax.psum_scatter(
            head_acc.astype(jnp.bfloat16), "segment", scatter_dimension=0, tiled=True
        ).astype(jnp.float32),
        lax.psum_scatter(
            gain_columns.astype(jnp.bfloat16), "segment", scatter_dimension=0, tiled=True
        ).astype(jnp.float32),
        lax.psum_scatter(
            bias_columns.astype(jnp.bfloat16), "segment", scatter_dimension=0, tiled=True
        ).astype(jnp.float32),
    )
    wide_total, mid_total, head_total = lax.psum((wide_acc, mid_acc, head_part), "dp")
    return (
        logit_part,
        input_part,
        wide_total[None],
        mid_total.reshape(1, 9, half_width, narrow),
        gain_acc[None],
        bias_acc[None],
        gain_part,
        bias_part,
        head_total,
    )


def solution(mesh):
    return jax.shard_map(
        on_device,
        mesh=mesh,
        in_specs=(
            P("segment", "dp", None, None),
            P(None, "dp", None),
            P("segment", None, None),
            P("segment", None, None, None),
            P("segment", None),
            P("segment", None),
            P("segment", None),
            P("segment", None),
            P("segment", None),
            P(None, "dp", None, None),
            P(None, "dp", None),
        ),
        out_specs=(
            P("segment", "dp", None, None),
            P("segment", "dp", None, None),
            P("segment", None, None),
            P("segment", None, None, None),
            P("segment", None),
            P("segment", None),
            P("segment", None),
            P("segment", None),
            P("segment", None),
        ),
        check_vma=False,
    )
```

profile of v0, /device:TPU:0, one launch (start us, length us, event | category | flops | bytes accessed | tf_op | source)
XLA Modules:
  0.0 3607.5 jit_solution(12170240076575194713)
XLA Ops:
  38.0 62.4 %all-gather.2.cloned.1.call-done = bf16[8,1,256,2048]{3,2,1,0:T(8,128)(2,1)} async-done(((bf16[2,1,256,2048]{3,2,1,0:T(8,128)(2,1)}), bf16[8,1,256,2048]{3,2,1,0:T(8,128)(2,1)}) %all-gather.2.cloned.1.call-update) | async-done | bytes 8388624 | tf_op jit(solution)/shard_map/all_gather | solution.py:129
  111.2 1334.1 %while.74 = (s32[]{:T(128)}, bf16[256,2048]{1,0:T(8,128)(2,1)S(1)}, bf16[256,512]{1,0:T(8,128)(2,1)S(1)}, bf16[256,256]{1,0:T(8,128)(2,1)S(1)}, bf16[8,256,2048]...) while((s32[]{:T(128)}, bf16[256,2048]{1,0:T(8,128)(2,1)S(1)}, ...), condition=%wide.region_21.22_spmd, body=%wide.region_3.21_spmd.sunk | while | flops 1266769408 | bytes 70565912 | solution.py:251
  1457.7 1726.4 %while.75 = (s32[]{:T(128)}, bf16[256,2048]{1,0:T(8,128)(2,1)}, bf16[256,512]{1,0:T(8,128)(2,1)S(1)}, bf16[256,256]{1,0:T(8,128)(2,1)}, f32[2048,512]{1,0:T(8,12...) while((s32[]{:T(128)}, bf16[256,2048]{1,0:T(8,128)(2,1)}, ...), condition=%wide.region_42.43_spmd.clone, body=%wide.region_23.42_spmd.clone.sunk | while | flops 3688046848 | bytes 246338960 | solution.py:424
  1492.6 27.1 all-reduce.15
  1519.7 31.1 conditional.36
  1588.8 34.2 collective-permute-done.5
  1641.5 27.1 all-reduce.15
  1668.6 31.1 conditional.36
  1737.7 32.7 collective-permute-done.5
  1788.9 27.1 all-reduce.15
  1816.0 31.1 conditional.36
  1885.1 44.2 %collective-permute-done.5 = bf16[256,256]{1,0:T(8,128)(2,1)S(1)} collective-permute-done((bf16[256,256]{1,0:T(8,128)(2,1)}, bf16[256,256]{1,0:T(8,128)(2,1)S(1)}, u32[]{:S(2)}, u32[]{:S(2)}) %collective-permute-start.5) | collective-permute-done | bytes 131104 | tf_op jit(solution)/shard_map/while/body/eval_jaxpr/ppermute | solution.py:23
  1974.9 31.1 conditional.36
  2044.1 42.0 %collective-permute-done.5 = bf16[256,256]{1,0:T(8,128)(2,1)S(1)} collective-permute-done((bf16[256,256]{1,0:T(8,128)(2,1)}, bf16[256,256]{1,0:T(8,128)(2,1)S(1)}, u32[]{:S(2)}, u32[]{:S(2)}) %collective-permute-start.5) | collective-permute-done | bytes 131104 | tf_op jit(solution)/shard_map/while/body/eval_jaxpr/ppermute | solution.py:23
  2131.6 31.1 conditional.36
  2200.8 42.0 %collective-permute-done.5 = bf16[256,256]{1,0:T(8,128)(2,1)S(1)} collective-permute-done((bf16[256,256]{1,0:T(8,128)(2,1)}, bf16[256,256]{1,0:T(8,128)(2,1)S(1)}, u32[]{:S(2)}, u32[]{:S(2)}) %collective-permute-start.5) | collective-permute-done | bytes 131104 | tf_op jit(solution)/shard_map/while/body/eval_jaxpr/ppermute | solution.py:23
  2288.4 31.1 conditional.36
  2357.5 42.0 %collective-permute-done.5 = bf16[256,256]{1,0:T(8,128)(2,1)S(1)} collective-permute-done((bf16[256,256]{1,0:T(8,128)(2,1)}, bf16[256,256]{1,0:T(8,128)(2,1)S(1)}, u32[]{:S(2)}, u32[]{:S(2)}) %collective-permute-start.5) | collective-permute-done | bytes 131104 | tf_op jit(solution)/shard_map/while/body/eval_jaxpr/ppermute | solution.py:23
  2445.1 31.1 conditional.36
  2514.2 42.0 %collective-permute-done.5 = bf16[256,256]{1,0:T(8,128)(2,1)S(1)} collective-permute-done((bf16[256,256]{1,0:T(8,128)(2,1)}, bf16[256,256]{1,0:T(8,128)(2,1)S(1)}, u32[]{:S(2)}, u32[]{:S(2)}) %collective-permute-start.5) | collective-permute-done | bytes 131104 | tf_op jit(solution)/shard_map/while/body/eval_jaxpr/ppermute | solution.py:23
  2601.8 31.1 conditional.36
  2670.9 42.0 %collective-permute-done.5 = bf16[256,256]{1,0:T(8,128)(2,1)S(1)} collective-permute-done((bf16[256,256]{1,0:T(8,128)(2,1)}, bf16[256,256]{1,0:T(8,128)(2,1)S(1)}, u32[]{:S(2)}, u32[]{:S(2)}) %collective-permute-start.5) | collective-permute-done | bytes 131104 | tf_op jit(solution)/shard_map/while/body/eval_jaxpr/ppermute | solution.py:23
  2758.5 31.1 conditional.36
  2827.6 42.0 %collective-permute-done.5 = bf16[256,256]{1,0:T(8,128)(2,1)S(1)} collective-permute-done((bf16[256,256]{1,0:T(8,128)(2,1)}, bf16[256,256]{1,0:T(8,128)(2,1)S(1)}, u32[]{:S(2)}, u32[]{:S(2)}) %collective-permute-start.5) | collective-permute-done | bytes 131104 | tf_op jit(solution)/shard_map/while/body/eval_jaxpr/ppermute | solution.py:23
  2915.2 31.1 conditional.36
  2984.3 42.0 %collective-permute-done.5 = bf16[256,256]{1,0:T(8,128)(2,1)S(1)} collective-permute-done((bf16[256,256]{1,0:T(8,128)(2,1)}, bf16[256,256]{1,0:T(8,128)(2,1)S(1)}, u32[]{:S(2)}, u32[]{:S(2)}) %collective-permute-start.5) | collective-permute-done | bytes 131104 | tf_op jit(solution)/shard_map/while/body/eval_jaxpr/ppermute | solution.py:23
  3071.9 31.1 conditional.36
  3141.1 41.9 %collective-permute-done.5 = bf16[256,256]{1,0:T(8,128)(2,1)S(1)} collective-permute-done((bf16[256,256]{1,0:T(8,128)(2,1)}, bf16[256,256]{1,0:T(8,128)(2,1)S(1)}, u32[]{:S(2)}, u32[]{:S(2)}) %collective-permute-start.5) | collective-permute-done | bytes 131104 | tf_op jit(solution)/shard_map/while/body/eval_jaxpr/ppermute | solution.py:23
  3190.8 43.0 %reduce-scatter.16.cloned.1.call-done = bf16[512,2]{1,0:T(8,128)(2,1)} async-done(((bf16[2048,2]{1,0:T(8,128)(2,1)}), bf16[512,2]{1,0:T(8,128)(2,1)}) %reduce-scatter.16.cloned.1.call-update) | async-done | bytes 2064
  3315.0 30.1 all-reduce.21
  3345.0 59.2 %reduce-scatter.12.cloned.1.call-done = bf16[2,1,256,2048]{3,2,1,0:T(8,128)(2,1)} async-done(((bf16[8,1,256,2048]{3,2,1,0:T(8,128)(2,1)}), bf16[2,1,256,2048]{3,2,1,0:T(8,128)(2,1)}) %reduce-scatter.12.cloned.1.call-update) | async-done | bytes 2097168 | tf_op jit(solution)/shard_map/reduce_scatter | solution.py:434
  3408.4 184.9 %all-reduce.20.cloned.1.call-done = (f32[1,2048,512]{2,1,0:T(8,128)}, f32[1,9,256,512]{3,2,1,0:T(8,128)}) async-done(((f32[1,2048,512]{2,1,0:T(8,128)}, f32[1,9,256,512]{3,2,1,0:T(8,128)}), (f32[1,2048,512]{2,1,0:T(8,128)}, f32[1,9,256,512]{3,2,1,0:T(8,128)})) %all-reduce.20.cloned.1.call-update) | async-done | bytes 8912912 | tf_op jit(solution)/shard_map/psum | solution.py:453
  (2086 shorter events, 2849.1 us)
Async XLA Ops:
  7.2 93.1 %all-gather.2.cloned.1.call-start = ((), (), s32[]{:S(2)}) async-start(), calls=%async_computation.5 | async-start | bytes 10485760 | tf_op jit(solution)/shard_map/all_gather | solution.py:129
  8.0 3225.9 %reduce-scatter.16.cloned.1.call-start = ((), (), s32[]{:S(2)}) async-start(), calls=%async_computation.9 | async-start | bytes 655360
  1876.7 52.7 %collective-permute-start.3 = (bf16[256,2048]{1,0:T(8,128)(2,1)}, bf16[256,2048]{1,0:T(8,128)(2,1)S(1)}, u32[]{:S(2)}, u32[]{:S(2)}) collective-permute-start(bf16[256,2048]{1,0:T(8,128)(2,1)} %convert_element_type.252), channel_id=1, source_target_pairs={{8,0},{16,8},{24,16},{9,1},{17,9},{25,17},{10,2},{18,10},{26,18},{... | collective-permute-start | bytes 3145736 | tf_op jit(solution)/shard_map/while/body/eval_jaxpr/ppermute | solution.py:23
  1878.0 51.4 %collective-permute-start.4 = (bf16[256,512]{1,0:T(8,128)(2,1)}, bf16[256,512]{1,0:T(8,128)(2,1)S(1)}, u32[]{:S(2)}, u32[]{:S(2)}) collective-permute-start(bf16[256,512]{1,0:T(8,128)(2,1)} %get-tuple-element.2607), channel_id=1, source_target_pairs={{8,0},{16,8},{24,16},{9,1},{17,9},{25,17},{10,2},{18,10},{26,18},{... | collective-permute-start | bytes 786440 | tf_op jit(solution)/shard_map/while/body/eval_jaxpr/ppermute | solution.py:23
  1879.3 50.1 %collective-permute-start.5 = (bf16[256,256]{1,0:T(8,128)(2,1)}, bf16[256,256]{1,0:T(8,128)(2,1)S(1)}, u32[]{:S(2)}, u32[]{:S(2)}) collective-permute-start(bf16[256,256]{1,0:T(8,128)(2,1)} %copy-done.23), channel_id=1, source_target_pairs={{8,0},{16,8},{24,16},{9,1},{17,9},{25,17},{10,2},{18,10},{26,18},{... | collective-permute-start | bytes 393224 | tf_op jit(solution)/shard_map/while/body/eval_jaxpr/ppermute | solution.py:23
  2035.6 50.5 %collective-permute-start.3 = (bf16[256,2048]{1,0:T(8,128)(2,1)}, bf16[256,2048]{1,0:T(8,128)(2,1)S(1)}, u32[]{:S(2)}, u32[]{:S(2)}) collective-permute-start(bf16[256,2048]{1,0:T(8,128)(2,1)} %convert_element_type.252), channel_id=1, source_target_pairs={{8,0},{16,8},{24,16},{9,1},{17,9},{25,17},{10,2},{18,10},{26,18},{... | collective-permute-start | bytes 3145736 | tf_op jit(solution)/shard_map/while/body/eval_jaxpr/ppermute | solution.py:23
  2036.9 49.2 %collective-permute-start.4 = (bf16[256,512]{1,0:T(8,128)(2,1)}, bf16[256,512]{1,0:T(8,128)(2,1)S(1)}, u32[]{:S(2)}, u32[]{:S(2)}) collective-permute-start(bf16[256,512]{1,0:T(8,128)(2,1)} %get-tuple-element.2607), channel_id=1, source_target_pairs={{8,0},{16,8},{24,16},{9,1},{17,9},{25,17},{10,2},{18,10},{26,18},{... | collective-permute-start | bytes 786440 | tf_op jit(solution)/shard_map/while/body/eval_jaxpr/ppermute | solution.py:23
  2038.2 47.9 %collective-permute-start.5 = (bf16[256,256]{1,0:T(8,128)(2,1)}, bf16[256,256]{1,0:T(8,128)(2,1)S(1)}, u32[]{:S(2)}, u32[]{:S(2)}) collective-permute-start(bf16[256,256]{1,0:T(8,128)(2,1)} %copy-done.23), channel_id=1, source_target_pairs={{8,0},{16,8},{24,16},{9,1},{17,9},{25,17},{10,2},{18,10},{26,18},{... | collective-permute-start | bytes 393224 | tf_op jit(solution)/shard_map/while/body/eval_jaxpr/ppermute | solution.py:23
  2192.3 50.5 %collective-permute-start.3 = (bf16[256,2048]{1,0:T(8,128)(2,1)}, bf16[256,2048]{1,0:T(8,128)(2,1)S(1)}, u32[]{:S(2)}, u32[]{:S(2)}) collective-permute-start(bf16[256,2048]{1,0:T(8,128)(2,1)} %convert_element_type.252), channel_id=1, source_target_pairs={{8,0},{16,8},{24,16},{9,1},{17,9},{25,17},{10,2},{18,10},{26,18},{... | collective-permute-start | bytes 3145736 | tf_op jit(solution)/shard_map/while/body/eval_jaxpr/ppermute | solution.py:23
  2193.6 49.2 %collective-permute-start.4 = (bf16[256,512]{1,0:T(8,128)(2,1)}, bf16[256,512]{1,0:T(8,128)(2,1)S(1)}, u32[]{:S(2)}, u32[]{:S(2)}) collective-permute-start(bf16[256,512]{1,0:T(8,128)(2,1)} %get-tuple-element.2607), channel_id=1, source_target_pairs={{8,0},{16,8},{24,16},{9,1},{17,9},{25,17},{10,2},{18,10},{26,18},{... | collective-permute-start | bytes 786440 | tf_op jit(solution)/shard_map/while/body/eval_jaxpr/ppermute | solution.py:23
  2194.9 47.9 %collective-permute-start.5 = (bf16[256,256]{1,0:T(8,128)(2,1)}, bf16[256,256]{1,0:T(8,128)(2,1)S(1)}, u32[]{:S(2)}, u32[]{:S(2)}) collective-permute-start(bf16[256,256]{1,0:T(8,128)(2,1)} %copy-done.23), channel_id=1, source_target_pairs={{8,0},{16,8},{24,16},{9,1},{17,9},{25,17},{10,2},{18,10},{26,18},{... | collective-permute-start | bytes 393224 | tf_op jit(solution)/shard_map/while/body/eval_jaxpr/ppermute | solution.py:23
  2349.0 50.5 %collective-permute-start.3 = (bf16[256,2048]{1,0:T(8,128)(2,1)}, bf16[256,2048]{1,0:T(8,128)(2,1)S(1)}, u32[]{:S(2)}, u32[]{:S(2)}) collective-permute-start(bf16[256,2048]{1,0:T(8,128)(2,1)} %convert_element_type.252), channel_id=1, source_target_pairs={{8,0},{16,8},{24,16},{9,1},{17,9},{25,17},{10,2},{18,10},{26,18},{... | collective-permute-start | bytes 3145736 | tf_op jit(solution)/shard_map/while/body/eval_jaxpr/ppermute | solution.py:23
  2350.3 49.2 %collective-permute-start.4 = (bf16[256,512]{1,0:T(8,128)(2,1)}, bf16[256,512]{1,0:T(8,128)(2,1)S(1)}, u32[]{:S(2)}, u32[]{:S(2)}) collective-permute-start(bf16[256,512]{1,0:T(8,128)(2,1)} %get-tuple-element.2607), channel_id=1, source_target_pairs={{8,0},{16,8},{24,16},{9,1},{17,9},{25,17},{10,2},{18,10},{26,18},{... | collective-permute-start | bytes 786440 | tf_op jit(solution)/shard_map/while/body/eval_jaxpr/ppermute | solution.py:23
  2351.6 47.9 %collective-permute-start.5 = (bf16[256,256]{1,0:T(8,128)(2,1)}, bf16[256,256]{1,0:T(8,128)(2,1)S(1)}, u32[]{:S(2)}, u32[]{:S(2)}) collective-permute-start(bf16[256,256]{1,0:T(8,128)(2,1)} %copy-done.23), channel_id=1, source_target_pairs={{8,0},{16,8},{24,16},{9,1},{17,9},{25,17},{10,2},{18,10},{26,18},{... | collective-permute-start | bytes 393224 | tf_op jit(solution)/shard_map/while/body/eval_jaxpr/ppermute | solution.py:23
  2505.7 50.5 %collective-permute-start.3 = (bf16[256,2048]{1,0:T(8,128)(2,1)}, bf16[256,2048]{1,0:T(8,128)(2,1)S(1)}, u32[]{:S(2)}, u32[]{:S(2)}) collective-permute-start(bf16[256,2048]{1,0:T(8,128)(2,1)} %convert_element_type.252), channel_id=1, source_target_pairs={{8,0},{16,8},{24,16},{9,1},{17,9},{25,17},{10,2},{18,10},{26,18},{... | collective-permute-start | bytes 3145736 | tf_op jit(solution)/shard_map/while/body/eval_jaxpr/ppermute | solution.py:23
  2507.0 49.2 %collective-permute-start.4 = (bf16[256,512]{1,0:T(8,128)(2,1)}, bf16[256,512]{1,0:T(8,128)(2,1)S(1)}, u32[]{:S(2)}, u32[]{:S(2)}) collective-permute-start(bf16[256,512]{1,0:T(8,128)(2,1)} %get-tuple-element.2607), channel_id=1, source_target_pairs={{8,0},{16,8},{24,16},{9,1},{17,9},{25,17},{10,2},{18,10},{26,18},{... | collective-permute-start | bytes 786440 | tf_op jit(solution)/shard_map/while/body/eval_jaxpr/ppermute | solution.py:23
  2508.3 47.9 %collective-permute-start.5 = (bf16[256,256]{1,0:T(8,128)(2,1)}, bf16[256,256]{1,0:T(8,128)(2,1)S(1)}, u32[]{:S(2)}, u32[]{:S(2)}) collective-permute-start(bf16[256,256]{1,0:T(8,128)(2,1)} %copy-done.23), channel_id=1, source_target_pairs={{8,0},{16,8},{24,16},{9,1},{17,9},{25,17},{10,2},{18,10},{26,18},{... | collective-permute-start | bytes 393224 | tf_op jit(solution)/shard_map/while/body/eval_jaxpr/ppermute | solution.py:23
  2662.5 50.4 %collective-permute-start.3 = (bf16[256,2048]{1,0:T(8,128)(2,1)}, bf16[256,2048]{1,0:T(8,128)(2,1)S(1)}, u32[]{:S(2)}, u32[]{:S(2)}) collective-permute-start(bf16[256,2048]{1,0:T(8,128)(2,1)} %convert_element_type.252), channel_id=1, source_target_pairs={{8,0},{16,8},{24,16},{9,1},{17,9},{25,17},{10,2},{18,10},{26,18},{... | collective-permute-start | bytes 3145736 | tf_op jit(solution)/shard_map/while/body/eval_jaxpr/ppermute | solution.py:23
  2663.8 49.1 %collective-permute-start.4 = (bf16[256,512]{1,0:T(8,128)(2,1)}, bf16[256,512]{1,0:T(8,128)(2,1)S(1)}, u32[]{:S(2)}, u32[]{:S(2)}) collective-permute-start(bf16[256,512]{1,0:T(8,128)(2,1)} %get-tuple-element.2607), channel_id=1, source_target_pairs={{8,0},{16,8},{24,16},{9,1},{17,9},{25,17},{10,2},{18,10},{26,18},{... | collective-permute-start | bytes 786440 | tf_op jit(solution)/shard_map/while/body/eval_jaxpr/ppermute | solution.py:23
  2819.2 50.5 %collective-permute-start.3 = (bf16[256,2048]{1,0:T(8,128)(2,1)}, bf16[256,2048]{1,0:T(8,128)(2,1)S(1)}, u32[]{:S(2)}, u32[]{:S(2)}) collective-permute-start(bf16[256,2048]{1,0:T(8,128)(2,1)} %convert_element_type.252), channel_id=1, source_target_pairs={{8,0},{16,8},{24,16},{9,1},{17,9},{25,17},{10,2},{18,10},{26,18},{... | collective-permute-start | bytes 3145736 | tf_op jit(solution)/shard_map/while/body/eval_jaxpr/ppermute | solution.py:23
  2820.4 49.2 %collective-permute-start.4 = (bf16[256,512]{1,0:T(8,128)(2,1)}, bf16[256,512]{1,0:T(8,128)(2,1)S(1)}, u32[]{:S(2)}, u32[]{:S(2)}) collective-permute-start(bf16[256,512]{1,0:T(8,128)(2,1)} %get-tuple-element.2607), channel_id=1, source_target_pairs={{8,0},{16,8},{24,16},{9,1},{17,9},{25,17},{10,2},{18,10},{26,18},{... | collective-permute-start | bytes 786440 | tf_op jit(solution)/shard_map/while/body/eval_jaxpr/ppermute | solution.py:23
  2821.7 47.9 %collective-permute-start.5 = (bf16[256,256]{1,0:T(8,128)(2,1)}, bf16[256,256]{1,0:T(8,128)(2,1)S(1)}, u32[]{:S(2)}, u32[]{:S(2)}) collective-permute-start(bf16[256,256]{1,0:T(8,128)(2,1)} %copy-done.23), channel_id=1, source_target_pairs={{8,0},{16,8},{24,16},{9,1},{17,9},{25,17},{10,2},{18,10},{26,18},{... | collective-permute-start | bytes 393224 | tf_op jit(solution)/shard_map/while/body/eval_jaxpr/ppermute | solution.py:23
  2975.9 50.5 %collective-permute-start.3 = (bf16[256,2048]{1,0:T(8,128)(2,1)}, bf16[256,2048]{1,0:T(8,128)(2,1)S(1)}, u32[]{:S(2)}, u32[]{:S(2)}) collective-permute-start(bf16[256,2048]{1,0:T(8,128)(2,1)} %convert_element_type.252), channel_id=1, source_target_pairs={{8,0},{16,8},{24,16},{9,1},{17,9},{25,17},{10,2},{18,10},{26,18},{... | collective-permute-start | bytes 3145736 | tf_op jit(solution)/shard_map/while/body/eval_jaxpr/ppermute | solution.py:23
  2977.2 49.2 %collective-permute-start.4 = (bf16[256,512]{1,0:T(8,128)(2,1)}, bf16[256,512]{1,0:T(8,128)(2,1)S(1)}, u32[]{:S(2)}, u32[]{:S(2)}) collective-permute-start(bf16[256,512]{1,0:T(8,128)(2,1)} %get-tuple-element.2607), channel_id=1, source_target_pairs={{8,0},{16,8},{24,16},{9,1},{17,9},{25,17},{10,2},{18,10},{26,18},{... | collective-permute-start | bytes 786440 | tf_op jit(solution)/shard_map/while/body/eval_jaxpr/ppermute | solution.py:23
  2978.5 47.9 %collective-permute-start.5 = (bf16[256,256]{1,0:T(8,128)(2,1)}, bf16[256,256]{1,0:T(8,128)(2,1)S(1)}, u32[]{:S(2)}, u32[]{:S(2)}) collective-permute-start(bf16[256,256]{1,0:T(8,128)(2,1)} %copy-done.23), channel_id=1, source_target_pairs={{8,0},{16,8},{24,16},{9,1},{17,9},{25,17},{10,2},{18,10},{26,18},{... | collective-permute-start | bytes 393224 | tf_op jit(solution)/shard_map/while/body/eval_jaxpr/ppermute | solution.py:23
  3132.6 50.5 %collective-permute-start.3 = (bf16[256,2048]{1,0:T(8,128)(2,1)}, bf16[256,2048]{1,0:T(8,128)(2,1)S(1)}, u32[]{:S(2)}, u32[]{:S(2)}) collective-permute-start(bf16[256,2048]{1,0:T(8,128)(2,1)} %convert_element_type.252), channel_id=1, source_target_pairs={{8,0},{16,8},{24,16},{9,1},{17,9},{25,17},{10,2},{18,10},{26,18},{... | collective-permute-start | bytes 3145736 | tf_op jit(solution)/shard_map/while/body/eval_jaxpr/ppermute | solution.py:23
  3133.9 49.2 %collective-permute-start.4 = (bf16[256,512]{1,0:T(8,128)(2,1)}, bf16[256,512]{1,0:T(8,128)(2,1)S(1)}, u32[]{:S(2)}, u32[]{:S(2)}) collective-permute-start(bf16[256,512]{1,0:T(8,128)(2,1)} %get-tuple-element.2607), channel_id=1, source_target_pairs={{8,0},{16,8},{24,16},{9,1},{17,9},{25,17},{10,2},{18,10},{26,18},{... | collective-permute-start | bytes 786440 | tf_op jit(solution)/shard_map/while/body/eval_jaxpr/ppermute | solution.py:23
  3186.0 75.7 %reduce-scatter.18.cloned.1.call-start = ((), (), s32[]{:S(2)}) async-start(), calls=%async_computation.10 | async-start | bytes 655360
  3187.1 101.2 %reduce-scatter.10.cloned.1.call-start = ((), (), s32[]{:S(2)}) async-start(), calls=%async_computation.6 | async-start | bytes 245760 | tf_op jit(solution)/shard_map/reduce_scatter | solution.py:440
  3187.7 127.2 %reduce-scatter.14.cloned.1.call-start = ((), (), s32[]{:S(2)}) async-start(), calls=%async_computation.8 | async-start | bytes 245760 | tf_op jit(solution)/shard_map/reduce_scatter | solution.py:443
  3189.5 214.8 %reduce-scatter.12.cloned.1.call-start = ((), (), s32[]{:S(2)}) async-start(), calls=%async_computation.7 | async-start | bytes 10485760 | tf_op jit(solution)/shard_map/reduce_scatter | solution.py:434
  3190.1 403.2 %all-reduce.20.cloned.1.call-start = ((), (), s32[]{:S(2)}) async-start(), calls=%async_computation.11 | async-start | bytes 17825792 | tf_op jit(solution)/shard_map/psum | solution.py:453
  (382 other events, 5999.2 us)
Sparse Core Ops, SparseCore 0:
  9.9 90.4 all-gather.1
  3186.1 47.6 reduce-scatter.15
  3236.9 24.7 reduce-scatter.17
  3264.3 23.9 reduce-scatter.9
  3290.9 23.9 reduce-scatter.13
  3317.9 86.3 reduce-scatter.11
  3407.4 185.8 all-reduce.19
where the time goes:
time: 3640 us; the launch traced here: 3610 us
  blocking collectives  1120 us (31%)
  waiting for transfers between devices  931 us (26%)
  local copies, waits for them, and re-layouts  699 us (19%)
  other arithmetic  321 us (9%)
  starting transfers between devices  273 us (8%)
  matrix products  211 us (6%)
  loops' own time  39.8 us (1%)
    ppermute x66, waiting for transfers between devices, shifted(): return lax.ppermute(value, axis, pairs)  503 us
    psum x11, blocking collectives, backward_tick(): lax.psum((jnp.sum(out_grad, axis=0), jnp.sum(out_grad * wide_normed, axis...  298 us
    ppermute x66, starting transfers between devices, shifted(): return lax.ppermute(value, axis, pairs)  273 us
    psum x1, waiting for transfers between devices, on_device(): lax.psum((wide_acc, mid_acc, head_part), 'dp')  185 us
    psum x11, blocking collectives, narrow_moments(): lax.psum((jnp.sum(values * mask_column, axis=0), local_count), 'dp')  160 us
    psum x11, blocking collectives, wide_moments(): summed = lax.psum(jnp.sum(values * mask_column, axis=0), 'dp')  153 us
    psum x11, blocking collectives, wide_moments(): spread = lax.psum(jnp.sum(centered * centered * mask_column, axis=0), 'dp')  153 us
    psum x11, blocking collectives, narrow_moments(): spread = lax.psum(jnp.sum(centered * centered * mask_column, axis=0), 'dp')  149 us
  transfers between devices with their start and end apart: 73, of which 29 were waited for; matrix products, arithmetic and copies ran while one was open for 5% of the time, Pallas kernels for 0%

commit v1 on v0

v1 whole, which is shorter than its diff:
```python
import jax
import jax.numpy as jnp
from jax import lax
from jax.sharding import PartitionSpec as P

KSEG = 40
KDEP = 1
KNOR = 3
FRAME = 16
PIX = FRAME * FRAME
EPS = 1e-05
DROP_FLOOR = 0.01
DROP_SHARPNESS = 8.0
CODE_SCALE = 65536.0
SWAP = 4

f32 = jnp.float32
bf16 = jnp.bfloat16
rows_only = (((0,), (0,)), ((), ()))
last_only = (((1,), (1,)), ((), ()))


def flip(value, bits):
    count = lax.axis_size("dp")
    return lax.ppermute(value, "dp", [(i, i ^ bits) for i in range(count)])


def seg_send(value, pairs):
    return lax.ppermute(value, "segment", pairs)


def group_levels():
    count = lax.axis_size("dp")
    bits = [1 << k for k in range(count.bit_length() - 1)]
    bits = [b for b in bits if b != SWAP]
    levels = [(bits[0], bits[1], bits[0] | bits[1])]
    return levels + [(b,) for b in bits[2:]]


def group_sum(value):
    for level in group_levels():
        got = [flip(value, b) for b in level]
        if len(got) == 3:
            value = (value + got[0]) + (got[1] + got[2])
        else:
            value = value + got[0]
    return value


def group_moments(local_sum, local_square, counts):
    total, square = local_sum, local_square
    for level, parts in zip(group_levels(), counts):
        packed = jnp.stack([total, square])
        got = [packed] + [flip(packed, b) for b in level]
        whole = sum(parts)
        total_next = sum(g[0] for g in got)
        mean = total_next / whole
        square = sum(g[1] for g in got)
        for g, n in zip(got, parts):
            away = g[0] / n - mean
            square = square + away * away * n
        total = total_next
    return mean, lax.rsqrt(square / whole + EPS)


def silu_slope(values):
    part = jax.nn.sigmoid(values)
    return part * (1.0 + values * (1.0 - part))


def patches(source):
    rows, channels = source.shape
    framed = source.reshape(rows // PIX, FRAME, FRAME, channels)
    padded = jnp.pad(framed, ((0, 0), (1, 1), (1, 1), (0, 0)))
    pieces = [
        padded[:, r : r + FRAME, c : c + FRAME, :].reshape(rows, channels)
        for r in range(3)
        for c in range(3)
    ]
    return jnp.concatenate(pieces, axis=-1)


def drop_merge(grads, thresholds):
    total = grads[0] + grads[1] + grads[2]
    magnitude = sum(jnp.sqrt(g * g + DROP_FLOOR * DROP_FLOOR) for g in grads)
    purity = 0.5 * (1.0 + total / magnitude)
    keep = jax.nn.sigmoid((purity - thresholds) * DROP_SHARPNESS)
    merged = jnp.zeros_like(total)
    for g in grads:
        merged = merged + g * jnp.where(g > 0.0, keep, 1.0 - keep)
    return merged


def spread(half, source, segment_index):
    x, y, d = source ^ 1, source ^ 2, source ^ 3
    middle = half.shape[0] // 2
    over_x = seg_send(half, [(source, x)])
    over_y = seg_send(half, [(source, y)])
    upper = seg_send(over_x[:middle], [(x, d)])
    lower = seg_send(over_y[middle:], [(y, d)])
    mine = jnp.where(
        segment_index == source, half, over_x + over_y + jnp.concatenate([upper, lower], axis=0)
    )
    other = flip(mine, 1)
    is_odd = lax.axis_index("dp") % 2 == 1
    return jnp.where(
        is_odd, jnp.concatenate([other, mine], axis=0), jnp.concatenate([mine, other], axis=0)
    )


def my_half(value):
    rows = value.shape[0] // 2
    odd = lax.axis_index("dp") % 2
    return lax.dynamic_slice_in_dim(value, odd * rows, rows, 0)


def gather_back(grad, segment_index):
    rows = grad.shape[0]
    odd = lax.axis_index("dp") % 2
    low = grad.astype(bf16)
    half = rows // 2
    keep = lax.dynamic_slice_in_dim(grad, odd * half, half, 0)
    give = lax.dynamic_slice_in_dim(low, (1 - odd) * half, half, 0)
    summed = keep + flip(give, 1).astype(f32)
    return summed


def on_device(
    inputs,
    extents,
    wide_weight,
    mid_weight,
    narrow_gain,
    narrow_bias,
    expand_gain,
    expand_bias,
    head_weight,
    head_cotangent,
    drop_codes,
):
    seg = lax.axis_index("segment")
    dp = lax.axis_index("dp")
    swapped = (dp // SWAP) % 2
    channels = inputs.shape[-1]
    narrow = wide_weight.shape[-1]
    half_width = narrow // 2
    classes = head_weight.shape[-1]

    def traded(value):
        keep = lax.dynamic_index_in_dim(value, swapped, 0, keepdims=False)
        give = lax.dynamic_index_in_dim(value, 1 - swapped, 0, keepdims=False)
        return jnp.concatenate([keep, flip(give, SWAP)], axis=0)

    own = inputs.shape[0]
    start = seg * own
    entry = traded(inputs).reshape(-1, channels)
    rows = entry.shape[0]
    images = rows // PIX
    box = traded(lax.dynamic_slice_in_dim(extents, start, own, 0))
    cotangent = traded(lax.dynamic_slice_in_dim(head_cotangent, start, own, 0))
    codes = traded(lax.dynamic_slice_in_dim(drop_codes, start, own, 0))

    position = jnp.arange(PIX, dtype=jnp.int32)
    inside = (position // FRAME < box[:, 0:1]) & (position % FRAME < box[:, 1:2])
    mask = inside.astype(f32).reshape(rows, 1)
    local_count = jnp.sum(mask)
    counts = []
    running = local_count
    for level in group_levels():
        parts = [running] + [flip(running, b) for b in level]
        counts.append(parts)
        running = sum(parts)
    pixel_count = running

    packed = jnp.concatenate([expand_gain, expand_bias, head_weight], axis=1).T
    small = lax.all_gather(packed, "segment", axis=1, tiled=True).astype(f32)
    gain_wide, bias_wide = small[0:2], small[2:4]
    head_rows = small[4:].astype(bf16)
    slim = lax.all_gather(jnp.concatenate([narrow_gain, narrow_bias], axis=0), "segment", axis=0)
    gain_narrow = slim[:, 0].astype(f32)
    bias_narrow = slim[:, 1].astype(f32)

    sections = lax.axis_size("segment")
    wide_half = my_half(wide_weight[0])
    mid_half = my_half(mid_weight[0].reshape(-1, narrow))
    order = [("w", 0), ("m", 0), ("m", 1), ("w", 1), ("w", 2), ("m", 2), ("m", 3), ("w", 3)]
    full = {}
    for kind, source in order:
        full[kind, source] = spread(wide_half if kind == "w" else mid_half, source, seg)

    cot_rows = cotangent.transpose(1, 0, 2).reshape(classes, rows)
    bounds = ((0, KSEG), (KSEG, KSEG + KDEP), (KSEG + KDEP, KSEG + KDEP + KNOR))
    thresholds = (
        jnp.broadcast_to(codes[:, None, :], (images, PIX, channels)).reshape(rows, channels).astype(f32)
        + 0.5
    ) / CODE_SCALE
    task_grads = [
        lax.dot_general(cot_rows[a:b], head_rows[a:b], rows_only, preferred_element_type=f32)
        for a, b in bounds
    ]
    merged = drop_merge(task_grads, thresholds)

    def moments(values):
        local_sum = jnp.sum(values * mask, axis=0)
        centered = values - local_sum / local_count
        local_square = jnp.sum(centered * centered * mask, axis=0)
        return group_moments(local_sum, local_square, counts)

    def block_forward(entry, k):
        head, tail = 2 * k, 2 * k + 1
        z1 = jnp.dot(entry, full["w", head], preferred_element_type=f32)
        mean1, inv1 = moments(z1)
        n1 = (z1 - mean1) * inv1
        a1 = n1 * gain_narrow[head] + bias_narrow[head]
        hidden = (jax.nn.silu(a1) * mask).astype(bf16)
        lower, upper = patches(hidden[:, :half_width]), patches(hidden[:, half_width:])
        partial = jnp.dot(lower, full["m", head], preferred_element_type=f32)
        z2 = partial + jnp.dot(upper, full["m", tail], preferred_element_type=f32)
        mean2, inv2 = moments(z2)
        n2 = (z2 - mean2) * inv2
        a2 = n2 * gain_narrow[tail] + bias_narrow[tail]
        hidden2 = (jax.nn.silu(a2) * mask).astype(bf16)
        z3 = lax.dot_general(hidden2, full["w", tail], last_only, preferred_element_type=f32)
        mean3, inv3 = moments(z3)
        n3 = (z3 - mean3) * inv3
        s = n3 * gain_wide[k] + bias_wide[k] + entry.astype(f32)
        out = (jax.nn.silu(s) * mask).astype(bf16)
        return out, (entry, n1, inv1, a1, lower, upper, n2, inv2, a2, hidden2, n3, inv3, s)

    y0, kept0 = block_forward(entry, 0)
    y1, kept1 = block_forward(y0, 1)
    logits = lax.dot_general(head_rows, y1, last_only, preferred_element_type=f32)
    head_grad = lax.dot_general(cot_rows, y1, (((1,), (0,)), ((), ())), preferred_element_type=f32)

    sums = {}
    grads = {}

    def back(d, n, gain, inv, sum_d, sum_dn):
        return (
            mask * inv * (gain * d - (gain * sum_d + n * (gain * sum_dn)) / pixel_count)
        ).astype(bf16)

    def pair_sums(d, n):
        both = group_sum(jnp.stack([jnp.sum(d, axis=0), jnp.sum(d * n, axis=0)]))
        return both

    def conv_back(gradient_patches, kernel):
        flipped = kernel.reshape(9, half_width, narrow)[::-1].transpose(0, 2, 1)
        return jnp.dot(gradient_patches, flipped.reshape(9 * narrow, half_width), preferred_element_type=f32)

    def block_backward(dy, kept, k):
        head, tail = 2 * k, 2 * k + 1
        entry, n1, inv1, a1, lower, upper, n2, inv2, a2, hidden2, n3, inv3, s = kept
        ds = dy * mask * silu_slope(s)
        sums["wide", k] = pair_sums(ds, n3)
        dz3 = back(ds, n3, gain_wide[k], inv3, sums["wide", k][0], sums["wide", k][1])
        dh2 = jnp.dot(dz3, full["w", tail], preferred_element_type=f32)
        grads["w", tail] = lax.dot_general(dz3, hidden2, rows_only, preferred_element_type=f32)
        d2 = dh2 * mask * silu_slope(a2)
        sums["narrow", tail] = pair_sums(d2, n2)
        dz2 = back(d2, n2, gain_narrow[tail], inv2, sums["narrow", tail][0], sums["narrow", tail][1])
        dz2_patches = patches(dz2)
        dh = jnp.concatenate(
            [conv_back(dz2_patches, full["m", head]), conv_back(dz2_patches, full["m", tail])], axis=1
        )
        grads["m", tail] = lax.dot_general(upper, dz2, rows_only, preferred_element_type=f32)
        grads["m", head] = lax.dot_general(lower, dz2, rows_only, preferred_element_type=f32)
        d1 = dh * mask * silu_slope(a1)
        sums["narrow", head] = pair_sums(d1, n1)
        dz1 = back(d1, n1, gain_narrow[head], inv1, sums["narrow", head][0], sums["narrow", head][1])
        grads["w", head] = lax.dot_general(entry, dz1, rows_only, preferred_element_type=f32)
        return lax.dot_general(dz1, full["w", head], last_only, preferred_element_type=f32) + ds

    du1 = block_backward(merged, kept1, 1)
    du0 = block_backward(du1, kept0, 0)

    def reduce_section(kind, source):
        part = gather_back(grads[kind, source], seg)
        x, y, d = source ^ 1, source ^ 2, source ^ 3
        middle = part.shape[0] // 2
        low = part.astype(bf16)
        to_x = seg_send(low[:middle], [(d, x)])
        to_y = seg_send(low[middle:], [(d, y)])
        from_x_lower = seg_send(low[middle:], [(x, source)])
        from_y_upper = seg_send(low[:middle], [(y, source)])
        from_x_upper = seg_send((part[:middle] + to_x.astype(f32)).astype(bf16), [(x, source)])
        from_y_lower = seg_send((part[middle:] + to_y.astype(f32)).astype(bf16), [(y, source)])
        total = part + jnp.concatenate(
            [
                from_y_upper.astype(f32) + from_x_upper.astype(f32),
                from_x_lower.astype(f32) + from_y_lower.astype(f32),
            ],
            axis=0,
        )
        return total

    def all_chips(total):
        count = lax.axis_size("dp")
        bits = [1 << k for k in range(1, count.bit_length() - 1)]
        parts = total
        for b in bits:
            rows_half = parts.shape[0] // 2
            side = (dp // b) % 2
            keep = lax.dynamic_slice_in_dim(parts, side * rows_half, rows_half, 0)
            give = lax.dynamic_slice_in_dim(parts, (1 - side) * rows_half, rows_half, 0).astype(bf16)
            parts = keep + flip(give, b).astype(f32)
        low = parts.astype(bf16)
        for b in bits[::-1] + [1]:
            got = flip(low, b)
            side = (dp // b) % 2 == 1
            low = jnp.where(
                side, jnp.concatenate([got, low], axis=0), jnp.concatenate([low, got], axis=0)
            )
        return low.astype(f32)

    def owned(kind):
        out = None
        for source in range(sections):
            total = reduce_section(kind, source)
            out = total if out is None else jnp.where(seg == source, total, out)
        return all_chips(out)

    wide_grad = owned("w")
    mid_grad = owned("m")

    wide_sums = jnp.stack([sums["wide", 0], sums["wide", 1]])
    narrow_sums = jnp.stack([sums["narrow", i] for i in range(4)])
    flat = jnp.concatenate([wide_sums.reshape(-1, narrow), narrow_sums.reshape(-1, narrow)], axis=0)
    flat = flat + flip(flat, SWAP)
    flat = flat + seg_send(flat, [(i, i ^ 1) for i in range(sections)])
    flat = flat + seg_send(flat, [(i, i ^ 2) for i in range(sections)])
    wide_count = wide_sums.size // narrow
    wide_all = flat[:wide_count].reshape(2, 2, channels)
    narrow_all = lax.dynamic_index_in_dim(flat[wide_count:].reshape(sections, 2, narrow), seg, 0, keepdims=False)
    share = channels // sections
    wide_mine = lax.dynamic_slice_in_dim(wide_all, seg * share, share, 2)

    head_part = lax.psum_scatter(head_grad, "segment", scatter_dimension=1, tiled=True)
    head_out = lax.psum(head_part, "dp").T

    def returned(value):
        keep = value[: images // 2]
        got = flip(value[images // 2 :].astype(bf16), SWAP).astype(f32)
        first = jnp.where(swapped == 0, keep, got)
        second = jnp.where(swapped == 0, got, keep)
        return jnp.stack([first, second])

    logits_out = returned(logits.reshape(classes, images, PIX).transpose(1, 0, 2))
    input_grad = returned(du0.reshape(images, PIX, channels))

    return (
        logits_out,
        input_grad,
        wide_grad[None],
        mid_grad.reshape(1, 9, half_width, narrow),
        narrow_all[1:2],
        narrow_all[0:1],
        wide_mine[:, 1].T,
        wide_mine[:, 0].T,
        head_out,
    )


def solution(mesh):
    return jax.shard_map(
        on_device,
        mesh=mesh,
        in_specs=(
            P("segment", "dp", None, None),
            P(None, "dp", None),
            P("segment", None, None),
            P("segment", None, None, None),
            P("segment", None),
            P("segment", None),
            P("segment", None),
            P("segment", None),
            P("segment", None),
            P(None, "dp", None, None),
            P(None, "dp", None),
        ),
        out_specs=(
            P("segment", "dp", None, None),
            P("segment", "dp", None, None),
            P("segment", None, None),
            P("segment", None, None, None),
            P("segment", None),
            P("segment", None),
            P("segment", None),
            P("segment", None),
            P("segment", None),
        ),
        check_vma=False,
    )
```

time: 3640 us -> 773 us (0.21)
  blocking collectives: 1120 us -> 46 us
  waiting for transfers between devices: 931 us -> 227 us
  local copies, waits for them, and re-layouts: 699 us -> 97.7 us
  other arithmetic: 321 us -> 97.9 us
  matrix products: 211 us -> 60.4 us
  starting transfers between devices: 273 us -> 213 us
  loops' own time: 39.8 us -> 0 us
    psum x67 -> x0, blocking collectives: 1090 us -> none  [the longest x11 298 us: backward_tick(): lax.psum((jnp.sum(out_grad, axis=0), jnp.sum(out_grad * wide_normed, axis...]
    ppermute x66 -> x154, waiting for transfers between devices: 503 us -> 205 us  [the longest x72 115 us: flip(): return lax.ppermute(value, 'dp', [(i, i ^ bits) for i in range(count)])]
    dynamic_slice x187 -> x4, local copies, waits for them, and re-layouts: 215 us -> 5.43 us  [the longest x2 3.36 us: my_half(): return lax.dynamic_slice_in_dim(value, odd * rows, rows, 0)]
    psum x1, waiting for transfers between devices: 185 us -> 21.6 us  [on_device(): head_out = lax.psum(head_part, 'dp').T]
    dot_general x77 -> x28, matrix products: 211 us -> 60.4 us  [the longest x2 18.3 us: on_device(): lax.dot_general(cot_rows[a:b], head_rows[a:b], rows_only, preferred_eleme...]
    cond x341 -> x0, local copies, waits for them, and re-layouts: 113 us -> none
    reduce_scatter x3 -> x1, waiting for transfers between devices: 109 us -> 0.01 us  [on_device(): lax.psum_scatter(head_grad, 'segment', scatter_dimension=1, tiled=True)]
    another operation x185 -> x0, local copies, waits for them, and re-layouts: 107 us -> none
  transfers between devices with their start and end apart: 73 -> 156, of which waited for: 29 -> 44; matrix products, arithmetic and copies ran while one was open for 5% -> 28% of each run, Pallas kernels for 0% -> 0%
where the time goes in v1:
time: 773 us; the launch traced here: 764 us
  waiting for transfers between devices  227 us (29%)
  starting transfers between devices  213 us (28%)
  other arithmetic  97.9 us (13%)
  local copies, waits for them, and re-layouts  97.7 us (13%)
  matrix products  60.4 us (8%)
  blocking collectives  46 us (6%)
  between operations  21.3 us (3%)
    ppermute x82, starting transfers between devices, seg_send(): return lax.ppermute(value, 'segment', pairs)  150 us
    ppermute x72, waiting for transfers between devices, flip(): return lax.ppermute(value, 'dp', [(i, i ^ bits) for i in range(count)])  115 us
    ppermute x82, waiting for transfers between devices, seg_send(): return lax.ppermute(value, 'segment', pairs)  90.5 us
    ppermute x72, starting transfers between devices, flip(): return lax.ppermute(value, 'dp', [(i, i ^ bits) for i in range(count)])  62.8 us
    all_gather x1, blocking collectives, on_device(): lax.all_gather(jnp.concatenate([narrow_gain, narrow_bias], axis=0), 'segm...  38.8 us
    psum x1, waiting for transfers between devices, on_device(): head_out = lax.psum(head_part, 'dp').T  21.6 us
    unnamed x366, local copies, waits for them, and re-layouts  21 us
    dot_general x2, matrix products, on_device(): lax.dot_general(cot_rows[a:b], head_rows[a:b], rows_only, preferred_eleme...  18.3 us
  transfers between devices with their start and end apart: 156, of which 44 were waited for; matrix products, arithmetic and copies ran while one was open for 28% of the time, Pallas kernels for 0%

profile of v1, /device:TPU:0, one launch (start us, length us, event | category | flops | bytes accessed | tf_op | source)
XLA Modules:
  0.0 763.6 jit_solution(921117362238053426)
XLA Ops:
  53.7 9.7 %collective-permute-start.2 = (bf16[1024,512]{1,0:T(8,128)(2,1)}, bf16[1024,512]{1,0:T(8,128)(2,1)S(1)}, u32[]{:S(2)}, u32[]{:S(2)}) collective-permute-start(bf16[1024,512]{1,0:T(8,128)(2,1)} %dynamic-slice_bitcast_fusion), channel_id=1, source_target_pairs={{0,16},{1,17},{2,18},{3,19},{4,20},{5,21},{6,22},{7,23}} | collective-permute-start | bytes 3145736 | tf_op jit(solution)/shard_map/ppermute | solution.py:29
  63.4 11.4 %collective-permute-done.26 = bf16[1024,512]{1,0:T(8,128)(2,1)} collective-permute-done((bf16[1024,512]{1,0:T(8,128)(2,1)}, bf16[1024,512]{1,0:T(8,128)(2,1)}, u32[]{:S(2)}, u32[]{:S(2)}) %collective-permute-start.26) | collective-permute-done | bytes 1048608 | tf_op jit(solution)/shard_map/ppermute | solution.py:29
  76.3 18.4 %collective-permute-done = bf16[1,256,2048]{2,1,0:T(8,128)(2,1)} collective-permute-done((bf16[1,256,2048]{2,1,0:T(8,128)(2,1)}, bf16[1,256,2048]{2,1,0:T(8,128)(2,1)}, u32[]{:S(2)}, u32[]{:S(2)}) %collective-permute-start) | collective-permute-done | bytes 1048608 | tf_op jit(solution)/shard_map/ppermute | solution.py:25
  95.5 38.8 %all-gather.1 = bf16[4,2,512]{2,1,0:T(2,128)(2,1)S(1)} all-gather(bf16[1,2,512]{2,1,0:T(2,128)(2,1)S(1)} %maximum_bitcast_fusion.2), channel_id=2, replica_groups=mesh['segment'=4,'dp'=8] {'segment'}, dimensions={0}, use_global_device_ids=true | all-gather | bytes 10240 | tf_op jit(solution)/shard_map/all_gather | solution.py:179
  134.3 7.2 all_gather.9
  146.3 5.3 collective-permute-start.14
  151.6 7.2 collective-permute-start.13
  184.6 4.4 collective-permute-start.45
  198.6 5.2 collective-permute-start.28
  217.9 5.2 collective-permute-start.20
  331.0 15.5 %fusion.125 = (f32[2048]{0:T(1024)S(1)}, f32[2048]{0:T(1024)S(1)}, f32[512,2048]{1,0:T(8,128)}, bf16[512,2048]{1,0:T(8,128)(2,1)S(1)}) fusion(f32[2048]{0:T(1024)S(1)} %bitcast.396, f32[512,2048]{1,0:T(8,128)} %copy-done.2, f32[2048]{0:T(1024)S(1)} %bitcast.398, bf16[512,2048]{1,0:T(8,128)(2,1)} %copy-done.14, f32[2048]{0:T(1024)S(1)} %bitcast.423, ...), kind=kOutput, calls=%fused_computation.516 | convolution fusion | flops 60813312 | bytes 16875520 | tf_op jit(solution)/shard_map/dot_general | solution.py:198
  354.0 5.0 multiply_convert_fusion.1
  432.6 4.8 collective-permute-start.90
  450.7 5.3 collective-permute-done.87
  465.2 6.0 collective-permute-done.101
  476.8 7.5 collective-permute-done.120
  491.9 7.2 collective-permute-done.134
  503.5 10.0 %collective-permute-start.93 = (bf16[512,512]{1,0:T(8,128)(2,1)S(1)}, bf16[512,512]{1,0:T(8,128)(2,1)S(1)}, u32[]{:S(2)}, u32[]{:S(2)}) collective-permute-start(bf16[512,512]{1,0:T(8,128)(2,1)S(1)} %copy-done.88), channel_id=1, source_target_pairs={{0,16},{1,17},{2,18},{3,19},{4,20},{5,21},{6,22},{7,23}} | collective-permute-start | bytes 1572872 | tf_op jit(solution)/shard_map/ppermute | solution.py:29
  515.0 5.5 collective-permute-start.103
  522.1 7.6 collective-permute-done.98
  531.9 4.6 collective-permute-start.102
  546.2 9.9 %collective-permute-done.112 = bf16[512,512]{1,0:T(8,128)(2,1)S(1)} collective-permute-done((bf16[512,512]{1,0:T(8,128)(2,1)S(1)}, bf16[512,512]{1,0:T(8,128)(2,1)S(1)}, u32[]{:S(2)}, u32[]{:S(2)}) %collective-permute-start.112) | collective-permute-done | bytes 524320 | tf_op jit(solution)/shard_map/ppermute | solution.py:29
  566.0 5.3 collective-permute-start.131
  582.1 5.0 collective-permute-done.136
  602.5 4.7 collective-permute-done.140
  623.6 5.0 collective-permute-done.146
  636.4 7.5 collective-permute-done.114
  644.1 23.4 %collective-permute-done.147 = bf16[288,512]{1,0:T(8,128)(2,1)S(1)} collective-permute-done((bf16[288,512]{1,0:T(8,128)(2,1)S(1)}, bf16[288,512]{1,0:T(8,128)(2,1)S(1)}, u32[]{:S(2)}, u32[]{:S(2)}) %collective-permute-start.147) | collective-permute-done | bytes 294944 | tf_op jit(solution)/shard_map/ppermute | solution.py:25
  675.4 11.7 %collective-permute-done.148 = bf16[288,512]{1,0:T(8,128)(2,1)S(1)} collective-permute-done((bf16[288,512]{1,0:T(8,128)(2,1)S(1)}, bf16[288,512]{1,0:T(8,128)(2,1)S(1)}, u32[]{:S(2)}, u32[]{:S(2)}) %collective-permute-start.148) | collective-permute-done | bytes 294944 | tf_op jit(solution)/shard_map/ppermute | solution.py:25
  694.3 10.5 %collective-permute-done.116 = bf16[512,512]{1,0:T(8,128)(2,1)} collective-permute-done((bf16[512,512]{1,0:T(8,128)(2,1)S(1)}, bf16[512,512]{1,0:T(8,128)(2,1)}, u32[]{:S(2)}, u32[]{:S(2)}) %collective-permute-start.116) | collective-permute-done | bytes 524320 | tf_op jit(solution)/shard_map/ppermute | solution.py:25
  706.5 16.1 %collective-permute-done.149 = bf16[576,512]{1,0:T(8,128)(2,1)} collective-permute-done((bf16[576,512]{1,0:T(8,128)(2,1)S(1)}, bf16[576,512]{1,0:T(8,128)(2,1)}, u32[]{:S(2)}, u32[]{:S(2)}) %collective-permute-start.149) | collective-permute-done | bytes 589856 | tf_op jit(solution)/shard_map/ppermute | solution.py:25
  733.4 21.6 %all-reduce.8.cloned.1.call-done = f32[512,44]{0,1:T(8,128)} async-done(((f32[512,44]{0,1:T(8,128)}), f32[512,44]{0,1:T(8,128)}) %all-reduce.8.cloned.1.call-update) | async-done | bytes 90128 | tf_op jit(solution)/shard_map/psum | solution.py:339
  (888 shorter events, 429.6 us)
Async XLA Ops:
  7.2 687.1 %reduce-scatter.2.cloned.1.call-start = ((), (), s32[]{:S(2)}) async-start(), calls=%async_computation.1 | async-start | bytes 491520 | tf_op jit(solution)/shard_map/reduce_scatter | solution.py:338
  9.5 33.1 %collective-permute-start.35 = (bf16[1024,512]{1,0:T(8,128)(2,1)}, bf16[1024,512]{1,0:T(8,128)(2,1)S(1)}, u32[]{:S(2)}, u32[]{:S(2)}) collective-permute-start(bf16[1024,512]{1,0:T(8,128)(2,1)} %dynamic-slice_bitcast_fusion), channel_id=1, source_target_pairs={{16,0},{17,1},{18,2},{19,3},{20,4},{21,5},{22,6},{23,7}} | collective-permute-start | bytes 3145736 | tf_op jit(solution)/shard_map/ppermute | solution.py:29
  10.9 36.7 %collective-permute-start.34 = (bf16[1024,512]{1,0:T(8,128)(2,1)}, bf16[1024,512]{1,0:T(8,128)(2,1)}, u32[]{:S(2)}, u32[]{:S(2)}) collective-permute-start(bf16[1024,512]{1,0:T(8,128)(2,1)} %dynamic-slice_bitcast_fusion), channel_id=1, source_target_pairs={{16,24},{17,25},{18,26},{19,27},{20,28},{21,29},{22,30},{23,31}} | collective-permute-start | bytes 3145736 | tf_op jit(solution)/shard_map/ppermute | solution.py:29
  12.6 39.0 %collective-permute-start.56 = (bf16[1024,512]{1,0:T(8,128)(2,1)}, bf16[1024,512]{1,0:T(8,128)(2,1)}, u32[]{:S(2)}, u32[]{:S(2)}) collective-permute-start(bf16[1024,512]{1,0:T(8,128)(2,1)} %dynamic-slice_bitcast_fusion), channel_id=1, source_target_pairs={{24,8},{25,9},{26,10},{27,11},{28,12},{29,13},{30,14},{31,15}} | collective-permute-start | bytes 3145736 | tf_op jit(solution)/shard_map/ppermute | solution.py:29
  14.3 38.7 %collective-permute-start.55 = (bf16[1024,512]{1,0:T(8,128)(2,1)}, bf16[1024,512]{1,0:T(8,128)(2,1)}, u32[]{:S(2)}, u32[]{:S(2)}) collective-permute-start(bf16[1024,512]{1,0:T(8,128)(2,1)} %dynamic-slice_bitcast_fusion), channel_id=1, source_target_pairs={{24,16},{25,17},{26,18},{27,19},{28,20},{29,21},{30,22},{31,23}} | collective-permute-start | bytes 3145736 | tf_op jit(solution)/shard_map/ppermute | solution.py:29
  43.6 31.1 %collective-permute-start.26 = (bf16[1024,512]{1,0:T(8,128)(2,1)}, bf16[1024,512]{1,0:T(8,128)(2,1)}, u32[]{:S(2)}, u32[]{:S(2)}) collective-permute-start(bf16[1024,512]{1,0:T(8,128)(2,1)} %dynamic-slice_bitcast_fusion), channel_id=1, source_target_pairs={{8,0},{9,1},{10,2},{11,3},{12,4},{13,5},{14,6},{15,7}} | collective-permute-start | bytes 3145736 | tf_op jit(solution)/shard_map/ppermute | solution.py:29
  47.6 47.1 %collective-permute-start = (bf16[1,256,2048]{2,1,0:T(8,128)(2,1)}, bf16[1,256,2048]{2,1,0:T(8,128)(2,1)}, u32[]{:S(2)}, u32[]{:S(2)}) collective-permute-start(bf16[1,256,2048]{2,1,0:T(8,128)(2,1)} %get-tuple-element.76), channel_id=1, source_target_pairs={{0,4},{1,5},{2,6},{3,7},{4,0},{5,1},{6,2},{7,3},{8,12},{9,13},{10,... | collective-permute-start | bytes 3145736 | tf_op jit(solution)/shard_map/ppermute | solution.py:25
  51.6 93.3 %collective-permute-start.43 = (bf16[1152,512]{1,0:T(8,128)(2,1)}, bf16[1152,512]{1,0:T(8,128)(2,1)S(1)}, u32[]{:S(2)}, u32[]{:S(2)}) collective-permute-start(bf16[1152,512]{1,0:T(8,128)(2,1)} %constant_dynamic-slice_fusion.8), channel_id=1, source_target_pairs={{16,0},{17,1},{18,2},{19,3},{20,4},{21,5},{22,6},{23,7}} | collective-permute-start | bytes 3538952 | tf_op jit(solution)/shard_map/ppermute | solution.py:29
  52.9 93.3 %collective-permute-start.42 = (bf16[1152,512]{1,0:T(8,128)(2,1)}, bf16[1152,512]{1,0:T(8,128)(2,1)S(1)}, u32[]{:S(2)}, u32[]{:S(2)}) collective-permute-start(bf16[1152,512]{1,0:T(8,128)(2,1)} %constant_dynamic-slice_fusion.8), channel_id=1, source_target_pairs={{16,24},{17,25},{18,26},{19,27},{20,28},{21,29},{22,30},{23,31}} | collective-permute-start | bytes 3538952 | tf_op jit(solution)/shard_map/ppermute | solution.py:29
  53.7 87.8 %collective-permute-start.2 = (bf16[1024,512]{1,0:T(8,128)(2,1)}, bf16[1024,512]{1,0:T(8,128)(2,1)S(1)}, u32[]{:S(2)}, u32[]{:S(2)}) collective-permute-start(bf16[1024,512]{1,0:T(8,128)(2,1)} %dynamic-slice_bitcast_fusion), channel_id=1, source_target_pairs={{0,16},{1,17},{2,18},{3,19},{4,20},{5,21},{6,22},{7,23}} | collective-permute-start | bytes 3145736 | tf_op jit(solution)/shard_map/ppermute | solution.py:29
  74.8 68.5 %collective-permute-start.1 = (bf16[1024,512]{1,0:T(8,128)(2,1)}, bf16[1024,512]{1,0:T(8,128)(2,1)S(1)}, u32[]{:S(2)}, u32[]{:S(2)}) collective-permute-start(bf16[1024,512]{1,0:T(8,128)(2,1)} %dynamic-slice_bitcast_fusion), channel_id=1, source_target_pairs={{0,8},{1,9},{2,10},{3,11},{4,12},{5,13},{6,14},{7,15}} | collective-permute-start | bytes 3145736 | tf_op jit(solution)/shard_map/ppermute | solution.py:29
  94.7 56.9 %collective-permute-start.48 = (bf16[1152,512]{1,0:T(8,128)(2,1)}, bf16[1152,512]{1,0:T(8,128)(2,1)S(1)}, u32[]{:S(2)}, u32[]{:S(2)}) collective-permute-start(bf16[1152,512]{1,0:T(8,128)(2,1)} %constant_dynamic-slice_fusion.8), channel_id=1, source_target_pairs={{24,8},{25,9},{26,10},{27,11},{28,12},{29,13},{30,14},{31,15}} | collective-permute-start | bytes 3538952 | tf_op jit(solution)/shard_map/ppermute | solution.py:29
  145.0 28.7 %collective-permute-start.18 = (bf16[1152,512]{1,0:T(8,128)(2,1)}, bf16[1152,512]{1,0:T(8,128)(2,1)}, u32[]{:S(2)}, u32[]{:S(2)}) collective-permute-start(bf16[1152,512]{1,0:T(8,128)(2,1)} %constant_dynamic-slice_fusion.8), channel_id=1, source_target_pairs={{8,0},{9,1},{10,2},{11,3},{12,4},{13,5},{14,6},{15,7}} | collective-permute-start | bytes 3538952 | tf_op jit(solution)/shard_map/ppermute | solution.py:29
  146.3 28.9 %collective-permute-start.14 = (bf16[1152,512]{1,0:T(8,128)(2,1)}, bf16[1152,512]{1,0:T(8,128)(2,1)}, u32[]{:S(2)}, u32[]{:S(2)}) collective-permute-start(bf16[1152,512]{1,0:T(8,128)(2,1)} %constant_dynamic-slice_fusion.8), channel_id=1, source_target_pairs={{0,16},{1,17},{2,18},{3,19},{4,20},{5,21},{6,22},{7,23}} | collective-permute-start | bytes 3538952 | tf_op jit(solution)/shard_map/ppermute | solution.py:29
  151.6 32.9 %collective-permute-start.13 = (bf16[1152,512]{1,0:T(8,128)(2,1)}, bf16[1152,512]{1,0:T(8,128)(2,1)}, u32[]{:S(2)}, u32[]{:S(2)}) collective-permute-start(bf16[1152,512]{1,0:T(8,128)(2,1)} %constant_dynamic-slice_fusion.8), channel_id=1, source_target_pairs={{0,8},{1,9},{2,10},{3,11},{4,12},{5,13},{6,14},{7,15}} | collective-permute-start | bytes 3538952 | tf_op jit(solution)/shard_map/ppermute | solution.py:29
  184.6 33.3 %collective-permute-start.45 = (bf16[576,512]{1,0:T(8,128)(2,1)S(1)}, bf16[576,512]{1,0:T(8,128)(2,1)S(1)}, u32[]{:S(2)}, u32[]{:S(2)}) collective-permute-start(bf16[576,512]{1,0:T(8,128)(2,1)S(1)} %slice.873), channel_id=1, source_target_pairs={{0,8},{1,9},{2,10},{3,11},{4,12},{5,13},{6,14},{7,15}} | collective-permute-start | bytes 1769480 | tf_op jit(solution)/shard_map/ppermute | solution.py:29
  228.4 30.1 %collective-permute-start.30 = (bf16[1024,512]{1,0:T(8,128)(2,1)S(1)}, bf16[1024,512]{1,0:T(8,128)(2,1)S(1)}, u32[]{:S(2)}, u32[]{:S(2)}) collective-permute-start(bf16[1024,512]{1,0:T(8,128)(2,1)S(1)} %get-tuple-element.98), channel_id=1, source_target_pairs={{0,1},{1,0},{2,3},{3,2},{4,5},{5,4},{6,7},{7,6},{8,9},{9,8},{10,11... | collective-permute-start | bytes 3145736 | tf_op jit(solution)/shard_map/ppermute | solution.py:25
  253.2 39.3 %collective-permute-start.59 = (bf16[1024,512]{1,0:T(8,128)(2,1)S(1)}, bf16[1024,512]{1,0:T(8,128)(2,1)S(1)}, u32[]{:S(2)}, u32[]{:S(2)}) collective-permute-start(bf16[1024,512]{1,0:T(8,128)(2,1)S(1)} %get-tuple-element.97), channel_id=1, source_target_pairs={{0,1},{1,0},{2,3},{3,2},{4,5},{5,4},{6,7},{7,6},{8,9},{9,8},{10,11... | collective-permute-start | bytes 3145736 | tf_op jit(solution)/shard_map/ppermute | solution.py:25
  297.4 30.1 %collective-permute-start.62 = (f32[2,2048]{1,0:T(2,128)}, f32[2,2048]{1,0:T(2,128)}, u32[]{:S(2)}, u32[]{:S(2)}) collective-permute-start(f32[2,2048]{1,0:T(2,128)} %pad_maximum_fusion.5), channel_id=1, source_target_pairs={{0,3},{1,2},{2,1},{3,0},{4,7},{5,6},{6,5},{7,4},{8,11},{9,10},{10,... | collective-permute-start | bytes 49160 | tf_op jit(solution)/shard_map/ppermute | solution.py:25
  298.4 29.2 %collective-permute-start.61 = (f32[2,2048]{1,0:T(2,128)}, f32[2,2048]{1,0:T(2,128)}, u32[]{:S(2)}, u32[]{:S(2)}) collective-permute-start(f32[2,2048]{1,0:T(2,128)} %pad_maximum_fusion.5), channel_id=1, source_target_pairs={{0,2},{1,3},{2,0},{3,1},{4,6},{5,7},{6,4},{7,5},{8,10},{9,11},{10,... | collective-permute-start | bytes 49160 | tf_op jit(solution)/shard_map/ppermute | solution.py:25
  299.6 28.0 %collective-permute-start.60 = (f32[2,2048]{1,0:T(2,128)}, f32[2,2048]{1,0:T(2,128)}, u32[]{:S(2)}, u32[]{:S(2)}) collective-permute-start(f32[2,2048]{1,0:T(2,128)} %pad_maximum_fusion.5), channel_id=1, source_target_pairs={{0,1},{1,0},{2,3},{3,2},{4,5},{5,4},{6,7},{7,6},{8,9},{9,8},{10,11... | collective-permute-start | bytes 49160 | tf_op jit(solution)/shard_map/ppermute | solution.py:25
  352.1 403.0 %all-reduce.8.cloned.1.call-start = ((), (), s32[]{:S(2)}) async-start(), calls=%async_computation.2 | async-start | bytes 196608 | tf_op jit(solution)/shard_map/psum | solution.py:339
  365.8 60.4 %collective-permute-start.85 = (bf16[1024,512]{1,0:T(8,128)(2,1)}, bf16[1024,512]{1,0:T(8,128)(2,1)}, u32[]{:S(2)}, u32[]{:S(2)}) collective-permute-start(bf16[1024,512]{1,0:T(8,128)(2,1)} %dynamic-slice_convert_fusion.7), channel_id=1, source_target_pairs={{0,1},{1,0},{2,3},{3,2},{4,5},{5,4},{6,7},{7,6},{8,9},{9,8},{10,11... | collective-permute-start | bytes 3145736 | tf_op jit(solution)/shard_map/ppermute | solution.py:25
  380.4 58.2 %collective-permute-start.118 = (bf16[1152,512]{1,0:T(8,128)(2,1)}, bf16[1152,512]{1,0:T(8,128)(2,1)}, u32[]{:S(2)}, u32[]{:S(2)}) collective-permute-start(bf16[1152,512]{1,0:T(8,128)(2,1)} %dynamic-slice_convert_fusion.3), channel_id=1, source_target_pairs={{0,1},{1,0},{2,3},{3,2},{4,5},{5,4},{6,7},{7,6},{8,9},{9,8},{10,11... | collective-permute-start | bytes 3538952 | tf_op jit(solution)/shard_map/ppermute | solution.py:25
  438.7 64.3 %collective-permute-start.89 = (bf16[512,512]{1,0:T(8,128)(2,1)}, bf16[512,512]{1,0:T(8,128)(2,1)S(1)}, u32[]{:S(2)}, u32[]{:S(2)}) collective-permute-start(bf16[512,512]{1,0:T(8,128)(2,1)} %get-tuple-element.95), channel_id=1, source_target_pairs={{16,24},{17,25},{18,26},{19,27},{20,28},{21,29},{22,30},{23,31}} | collective-permute-start | bytes 1572872 | tf_op jit(solution)/shard_map/ppermute | solution.py:29
  593.9 94.1 %collective-permute-start.63 = (bf16[1,44,256]{2,0,1:T(2,128)(2,1)}, bf16[1,44,256]{2,0,1:T(2,128)(2,1)S(1)}, u32[]{:S(2)}, u32[]{:S(2)}) collective-permute-start(bf16[1,44,256]{2,0,1:T(2,128)(2,1)} %slice.1237), channel_id=1, source_target_pairs={{0,4},{1,5},{2,6},{3,7},{4,0},{5,1},{6,2},{7,3},{8,12},{9,13},{10,... | collective-permute-start | bytes 67592 | tf_op jit(solution)/shard_map/ppermute | solution.py:25
  612.3 58.6 %collective-permute-start.151 = (f32[24,512]{1,0:T(8,128)S(1)}, f32[24,512]{1,0:T(8,128)S(1)}, u32[]{:S(2)}, u32[]{:S(2)}) collective-permute-start(f32[24,512]{1,0:T(8,128)S(1)} %constant_dynamic-update-slice_fusion.54), channel_id=1, source_target_pairs={{0,4},{1,5},{2,6},{3,7},{4,0},{5,1},{6,2},{7,3},{8,12},{9,13},{10,... | collective-permute-start | bytes 147464 | tf_op jit(solution)/shard_map/ppermute | solution.py:25
  629.9 37.6 %collective-permute-start.147 = (bf16[288,512]{1,0:T(8,128)(2,1)S(1)}, bf16[288,512]{1,0:T(8,128)(2,1)S(1)}, u32[]{:S(2)}, u32[]{:S(2)}) collective-permute-start(bf16[288,512]{1,0:T(8,128)(2,1)S(1)} %dynamic-slice_convert_fusion.10), channel_id=1, source_target_pairs={{0,4},{1,5},{2,6},{3,7},{4,0},{5,1},{6,2},{7,3},{8,12},{9,13},{10,... | collective-permute-start | bytes 884744 | tf_op jit(solution)/shard_map/ppermute | solution.py:25
  644.1 30.4 %collective-permute-start.115 = (bf16[256,512]{1,0:T(8,128)(2,1)S(1)}, bf16[256,512]{1,0:T(8,128)(2,1)S(1)}, u32[]{:S(2)}, u32[]{:S(2)}) collective-permute-start(bf16[256,512]{1,0:T(8,128)(2,1)S(1)} %add_convert_fusion.1), channel_id=1, source_target_pairs={{0,4},{1,5},{2,6},{3,7},{4,0},{5,1},{6,2},{7,3},{8,12},{9,13},{10,... | collective-permute-start | bytes 786440 | tf_op jit(solution)/shard_map/ppermute | solution.py:25
  667.8 56.5 %collective-permute-start.84 = (bf16[1,256,2048]{2,1,0:T(8,128)(2,1)S(1)}, bf16[1,256,2048]{2,1,0:T(8,128)(2,1)S(1)}, u32[]{:S(2)}, u32[]{:S(2)}) collective-permute-start(bf16[1,256,2048]{2,1,0:T(8,128)(2,1)S(1)} %fusion.39), channel_id=1, source_target_pairs={{0,4},{1,5},{2,6},{3,7},{4,0},{5,1},{6,2},{7,3},{8,12},{9,13},{10,... | collective-permute-start | bytes 3145736 | tf_op jit(solution)/shard_map/ppermute | solution.py:25
  674.7 30.1 %collective-permute-start.116 = (bf16[512,512]{1,0:T(8,128)(2,1)S(1)}, bf16[512,512]{1,0:T(8,128)(2,1)}, u32[]{:S(2)}, u32[]{:S(2)}) collective-permute-start(bf16[512,512]{1,0:T(8,128)(2,1)S(1)} %maximum_select_fusion.13), channel_id=1, source_target_pairs={{0,2},{1,3},{2,0},{3,1},{4,6},{5,7},{6,4},{7,5},{8,10},{9,11},{10,... | collective-permute-start | bytes 1572872 | tf_op jit(solution)/shard_map/ppermute | solution.py:25
  687.3 35.2 %collective-permute-start.149 = (bf16[576,512]{1,0:T(8,128)(2,1)S(1)}, bf16[576,512]{1,0:T(8,128)(2,1)}, u32[]{:S(2)}, u32[]{:S(2)}) collective-permute-start(bf16[576,512]{1,0:T(8,128)(2,1)S(1)} %maximum_select_fusion.12), channel_id=1, source_target_pairs={{0,2},{1,3},{2,0},{3,1},{4,6},{5,7},{6,4},{7,5},{8,10},{9,11},{10,... | collective-permute-start | bytes 1769480 | tf_op jit(solution)/shard_map/ppermute | solution.py:25
  (279 other events, 3807.2 us)
Sparse Core Ops, SparseCore 0:
  352.2 26.1 reduce-scatter.1
  694.4 60.6 all-reduce.7

commit v2 on v1

v2 whole, which is shorter than its diff:
```python
import functools

import jax
import jax.numpy as jnp
from jax import lax
from jax.experimental import pallas as pl
from jax.experimental.pallas import tpu as pltpu
from jax.sharding import PartitionSpec as P

KSEG = 40
KDEP = 1
KNOR = 3
FRAME = 16
PIX = FRAME * FRAME
EPS = 1e-05
DROP_FLOOR = 0.01
DROP_SHARPNESS = 8.0
CODE_SCALE = 65536.0
SWAP = 2
STEP = 64
PAD = FRAME
HEADS = 64
LIMIT = 24 << 20

f32 = jnp.float32
bf16 = jnp.bfloat16
rows_only = (((0,), (0,)), ((), ()))
last_only = (((1,), (1,)), ((), ()))


def sigmoid(values):
    return 0.5 * jnp.tanh(0.5 * values) + 0.5


def fold(values):
    return jnp.sum(values.reshape(values.shape[0] // 8, 8, values.shape[1]), axis=0)


def over_rows(rows, body, init):
    def one(index, carry):
        return body(pl.ds(pl.multiple_of(index * STEP, STEP), STEP), carry)

    return lax.fori_loop(0, rows // STEP, one, init)


def column_sum(total):
    return jnp.sum(total, axis=0, keepdims=True)


def local_moments(z_ref, cols, mask_ref, count, st_ref):
    rows, width = z_ref.shape[0], cols.size
    zero = jnp.zeros((8, width), f32)

    def add(r, total):
        return total + fold(z_ref[r, cols] * mask_ref[r, :])

    total = column_sum(over_rows(rows, add, zero))
    mean = total / count

    def add_square(r, square):
        away = z_ref[r, cols] - mean
        return square + fold(away * away * mask_ref[r, :])

    square = column_sum(over_rows(rows, add_square, zero))
    st_ref[0:1, cols] = total
    st_ref[1:2, cols] = square
    if st_ref.shape[0] > 2:
        st_ref[2:3, cols] = jnp.zeros_like(total) + count


def pixels(counts):
    numbers = [c[0:1, 0:1] for c in counts]
    return numbers, (numbers[0] + numbers[1]) + (numbers[2] + numbers[3])


def merged_moments(parts, counts, mi_ref):
    numbers, whole = pixels(counts)
    sums = [p[0:1, :] for p in parts]
    squares = [p[1:2, :] for p in parts]
    mean = ((sums[0] + sums[1]) + (sums[2] + sums[3])) / whole
    square = (squares[0] + squares[1]) + (squares[2] + squares[3])
    for s, n in zip(sums, numbers):
        away = s / n - mean
        square = square + away * away * n
    mi_ref[0:1, :] = mean
    mi_ref[1:2, :] = lax.rsqrt(square / whole + EPS)


def merged_sums(parts, out_ref):
    out_ref[...] = (parts[0][...] + parts[1][...]) + (parts[2][...] + parts[3][...])


class Weights:
    def __init__(self, section, place_ref, sources, buffer, sems):
        self.buffer, self.sems = buffer, sems
        self.piece = buffer.shape[0] // 4
        self.own = own = sources[0]
        first, second, third, other_first, other_second, other_third = sources[1:]
        relative = place_ref[0] ^ section
        core = place_ref[1]
        straight = relative == 1 + core
        near = (relative == 1) | (relative == 2)

        @pl.when(relative == 0)
        def _():
            for i in range(4):
                pltpu.make_async_copy(own.at[pl.ds(i * self.piece, self.piece)], self.part(i), sems.at[i]).start()

        def fetch(mine, other):
            for i in range(4):
                source, side = (mine, core) if i < 2 else (other, 1 - core)
                at = side * 2 + i % 2
                rows = pl.ds(i % 2 * self.piece, self.piece)
                pltpu.make_async_copy(source.at[rows], self.part(at), sems.at[at]).start()

        @pl.when(near & straight)
        def _():
            fetch(first, other_second)

        @pl.when(near & jnp.logical_not(straight))
        def _():
            fetch(second, other_first)

        @pl.when(relative == 3)
        def _():
            fetch(third, other_third)

    def part(self, at):
        start = at * self.piece
        if not isinstance(at, int):
            start = pl.multiple_of(start, 16)
        return self.buffer.at[pl.ds(start, self.piece)]

    def wait(self, at):
        source = self.own.at[pl.ds(0, self.piece)]
        pltpu.make_async_copy(source, self.part(at), self.sems.at[at]).wait()


def blocks(width, count=4):
    size = width // count
    return [pl.ds(i * size, size) for i in range(count)]


def first_kernel(section, place, k0, u, mask, *rest):
    sources, (z, st, w, sems) = rest[:7], rest[7:]
    weights = Weights(section, place, sources, w, sems)
    for i, cols in enumerate(blocks(u.shape[1])):
        weights.wait(i)
        part = jnp.dot(u[:, cols], w[cols, :], preferred_element_type=f32)
        z[...] = part if i == 0 else z[...] + part
    local_moments(z, pl.ds(0, z.shape[1]), mask, k0[0:1, 0:1], st)


def shifted_copies(values, column):
    left = jnp.where(column >= 1, pltpu.roll(values, 1, 0), 0.0)
    right = jnp.where(column < FRAME - 1, pltpu.roll(values, PIX - 1, 0), 0.0)
    return left, values, right


def clear_borders(buffer):
    images, rows, width = buffer.shape
    zero = jnp.zeros((images, PAD, width), bf16)
    buffer[:, 0:PAD, :] = zero
    buffer[:, rows - PAD : rows, :] = zero


def frame_column(width):
    return lax.broadcasted_iota(jnp.int32, (PIX, width), 0) % FRAME


def middle_kernel(section, place, k0, k1, k2, k3, z1, p0, p1, p2, p3, gain, bias, mask, *rest):
    sources, (hs, z2, st, mi, ka, kt, sems_a, sems_t) = rest[:7], rest[7:]
    lower = Weights(section, place, sources, ka, sems_a)
    upper = Weights(section + 1, place, sources, kt, sems_t)
    merged_moments((p0, p1, p2, p3), (k0, k1, k2, k3), mi)
    clear_borders(hs)
    images = hs.shape[0]
    half = z1.shape[1] // 2
    column = frame_column(128)

    def one(image, carry):
        r = pl.ds(pl.multiple_of(image * PIX, PIX), PIX)
        for j in range(z1.shape[1] // 128):
            cols = pl.ds(j * 128, 128)
            n = (z1[r, cols] - mi[0:1, cols]) * mi[1:2, cols]
            a = n * gain[:, cols] + bias[:, cols]
            h = a * sigmoid(a) * mask[r, :]
            side, inner = divmod(j * 128, half)
            for k, copy in enumerate(shifted_copies(h, column)):
                hs[image, PAD : PAD + PIX, pl.ds(side * 3 * half + k * half + inner, 128)] = copy.astype(bf16)
        return carry

    lax.fori_loop(0, images, one, 0)
    for weights in (lower, upper):
        for i in range(4):
            weights.wait(i)
    rows = z1.shape[0]
    for d in range(3):
        taps = hs[:, FRAME * d : FRAME * d + PIX, :].reshape(rows, 6 * half)
        ks = pl.ds(3 * half * d, 3 * half)
        part = jnp.dot(taps[:, : 3 * half], ka[ks, :], preferred_element_type=f32)
        part = part + jnp.dot(taps[:, 3 * half :], kt[ks, :], preferred_element_type=f32)
        z2[...] = part if d == 0 else z2[...] + part
    local_moments(z2, pl.ds(0, z2.shape[1]), mask, k0[0:1, 0:1], st)


def expand_kernel(section, place, k0, k1, k2, k3, z2, p0, p1, p2, p3, gain, bias, mask, *rest):
    sources, (h2, z3, st, mi, w, sems) = rest[:7], rest[7:]
    weights = Weights(section, place, sources, w, sems)
    merged_moments((p0, p1, p2, p3), (k0, k1, k2, k3), mi)

    def one(r, carry):
        n = (z2[r, :] - mi[0:1, :]) * mi[1:2, :]
        a = n * gain[...] + bias[...]
        h2[r, :] = (a * sigmoid(a) * mask[r, :]).astype(bf16)
        return carry

    over_rows(z2.shape[0], one, 0)
    for i, cols in enumerate(blocks(z3.shape[1])):
        weights.wait(i)
        z3[:, cols] = lax.dot_general(h2[...], w[cols, :], last_only, preferred_element_type=f32)
        local_moments(z3, cols, mask, k0[0:1, 0:1], st)


def join_kernel(section, place, k0, k1, k2, k3, z3, p0, p1, p2, p3, gain, bias, u, mask, *rest):
    sources, (y, z, st, mi, w, sems) = rest[:7], rest[7:]
    weights = Weights(section, place, sources, w, sems)
    merged_moments((p0, p1, p2, p3), (k0, k1, k2, k3), mi)
    for i, cols in enumerate(blocks(z3.shape[1])):

        def one(r, carry, cols=cols):
            n = (z3[r, cols] - mi[0:1, cols]) * mi[1:2, cols]
            s = n * gain[:, cols] + bias[:, cols] + u[r, cols].astype(f32)
            y[r, cols] = (s * sigmoid(s) * mask[r, :]).astype(bf16)
            return carry

        over_rows(z3.shape[0], one, 0)
        weights.wait(i)
        part = jnp.dot(y[:, cols], w[cols, :], preferred_element_type=f32)
        z[...] = part if i == 0 else z[...] + part
    local_moments(z, pl.ds(0, z.shape[1]), mask, k0[0:1, 0:1], st)


def slope_of(s):
    part = sigmoid(s)
    return part, part * (1.0 + s * (1.0 - part))


def turn_kernel(k0, k1, k2, k3, z3, p0, p1, p2, p3, gain, bias, u, mask, merged, head, cot, ds, n3, sums, logits, hgrad, mi, y):
    merged_moments((p0, p1, p2, p3), (k0, k1, k2, k3), mi)
    for i, cols in enumerate(blocks(z3.shape[1])):
        width = cols.size

        def one(r, carry, cols=cols):
            n = (z3[r, cols] - mi[0:1, cols]) * mi[1:2, cols]
            s = n * gain[:, cols] + bias[:, cols] + u[r, cols].astype(f32)
            part, slope = slope_of(s)
            y[r, :] = (s * part * mask[r, :]).astype(bf16)
            d = merged[r, cols].astype(f32) * mask[r, :] * slope
            ds[r, cols] = d.astype(bf16)
            n3[r, cols] = n.astype(bf16)
            return carry[0] + fold(d), carry[1] + fold(d * n)

        zero = jnp.zeros((8, width), f32)
        both = over_rows(z3.shape[0], one, (zero, zero))
        sums[0:1, cols] = column_sum(both[0])
        sums[1:2, cols] = column_sum(both[1])
        part = lax.dot_general(head[:, cols], y[...], last_only, preferred_element_type=f32)
        logits[...] = part if i == 0 else logits[...] + part
        for image in range(cot.shape[0]):
            r = pl.ds(image * PIX, PIX)
            part = jnp.dot(cot[image], y[r, :], preferred_element_type=f32)
            hgrad[:, cols] = part if image == 0 else hgrad[:, cols] + part


def shrink_kernel(section, place, number, ds, n3, q0, q1, q2, q3, mi3, gain3, mask, z2, mi2, gain2, bias2, *rest):
    sources, (dz3, d2, sums, tot, w, sems) = rest[:7], rest[7:]
    weights = Weights(section, place, sources, w, sems)
    merged_sums((q0, q1, q2, q3), tot)
    for i, cols in enumerate(blocks(ds.shape[1])):
        g = gain3[:, cols] * mi3[1:2, cols]
        c1 = g * tot[0:1, cols] / number[0:1, 0:1]
        c2 = g * tot[1:2, cols] / number[0:1, 0:1]

        def one(r, carry, cols=cols, g=g, c1=c1, c2=c2):
            d = g * ds[r, cols].astype(f32) - (c1 + n3[r, cols].astype(f32) * c2)
            dz3[r, cols] = (mask[r, :] * d).astype(bf16)
            return carry

        over_rows(ds.shape[0], one, 0)
        weights.wait(i)
        part = jnp.dot(dz3[:, cols], w[cols, :], preferred_element_type=f32)
        d2[...] = part if i == 0 else d2[...] + part
    narrow_back(d2, z2, mi2, gain2, bias2, mask, sums)


def narrow_back(d, z, mi, gain, bias, mask, sums):
    zero = jnp.zeros((8, z.shape[1]), f32)

    def one(r, carry):
        n = (z[r, :] - mi[0:1, :]) * mi[1:2, :]
        slope = slope_of(n * gain[...] + bias[...])[1]
        value = d[r, :] * mask[r, :] * slope
        d[r, :] = value
        return carry[0] + fold(value), carry[1] + fold(value * n)

    both = over_rows(z.shape[0], one, (zero, zero))
    sums[0:1, :] = column_sum(both[0])
    sums[1:2, :] = column_sum(both[1])


def unmix_kernel(section, place, number, d2, q0, q1, q2, q3, z2, mi2, gain2, mask, z1, mi1, gain1, bias1, *rest):
    sources, (dz2, d1, sums, tot, gs, ka, kt, sems_a, sems_t) = rest[:7], rest[7:]
    lower = Weights(section, place, sources, ka, sems_a)
    upper = Weights(section + 1, place, sources, kt, sems_t)
    merged_sums((q0, q1, q2, q3), tot)
    clear_borders(gs)
    images = gs.shape[0]
    rows, width = z2.shape
    half = width // 2
    column = frame_column(128)

    def one(image, carry):
        r = pl.ds(pl.multiple_of(image * PIX, PIX), PIX)
        for j in range(width // 128):
            cols = pl.ds(j * 128, 128)
            g = gain2[:, cols] * mi2[1:2, cols]
            c1 = g * tot[0:1, cols] / number[0:1, 0:1]
            c2 = g * tot[1:2, cols] / number[0:1, 0:1]
            n = (z2[r, cols] - mi2[0:1, cols]) * mi2[1:2, cols]
            d = mask[r, :] * (g * d2[r, cols] - (c1 + n * c2))
            dz2[r, cols] = d.astype(bf16)
            for k, copy in enumerate(shifted_copies(d, column)):
                gs[image, PAD : PAD + PIX, pl.ds(k * width + j * 128, 128)] = copy.astype(bf16)
        return carry

    lax.fori_loop(0, images, one, 0)
    for weights in (lower, upper):
        for i in range(4):
            weights.wait(i)
    for d in range(3):
        for k in range(3):
            moved = gs[:, FRAME * (2 - d) : FRAME * (2 - d) + PIX, pl.ds((2 - k) * width, width)]
            moved = moved.reshape(rows, width)
            tap = pl.ds((3 * d + k) * half, half)
            for side, kernel in enumerate((ka, kt)):
                cols = pl.ds(side * half, half)
                part = lax.dot_general(moved, kernel[tap, :], last_only, preferred_element_type=f32)
                d1[:, cols] = part if d + k == 0 else d1[:, cols] + part
    narrow_back(d1, z1, mi1, gain1, bias1, mask, sums)


def narrow_finish(d1, q, z1, mi1, gain1, mask, number, dz1, tot):
    merged_sums(q, tot)
    g = gain1[...] * mi1[1:2, :]
    c1 = g * tot[0:1, :] / number[0:1, 0:1]
    c2 = g * tot[1:2, :] / number[0:1, 0:1]

    def one(r, carry):
        n = (z1[r, :] - mi1[0:1, :]) * mi1[1:2, :]
        dz1[r, :] = (mask[r, :] * (g * d1[r, :] - (c1 + n * c2))).astype(bf16)
        return carry

    over_rows(z1.shape[0], one, 0)


def widen_kernel(section, place, number, d1, q0, q1, q2, q3, z1, mi1, gain1, mask, ds, z3, mi3, gain3, bias3, u, *rest):
    sources, (dz1, ds0, n3, sums, tot, w, du, sems) = rest[:7], rest[7:]
    weights = Weights(section, place, sources, w, sems)
    narrow_finish(d1, (q0, q1, q2, q3), z1, mi1, gain1, mask, number, dz1, tot)
    for i, cols in enumerate(blocks(ds.shape[1])):
        weights.wait(i)
        du[...] = lax.dot_general(dz1[...], w[cols, :], last_only, preferred_element_type=f32)

        def one(r, carry, cols=cols):
            dy = (du[r, :] + ds[r, cols].astype(f32)).astype(bf16).astype(f32)
            n = (z3[r, cols] - mi3[0:1, cols]) * mi3[1:2, cols]
            s = n * gain3[:, cols] + bias3[:, cols] + u[r, cols].astype(f32)
            d = dy * mask[r, :] * slope_of(s)[1]
            ds0[r, cols] = d.astype(bf16)
            n3[r, cols] = n.astype(bf16)
            return carry[0] + fold(d), carry[1] + fold(d * n)

        zero = jnp.zeros((8, cols.size), f32)
        both = over_rows(ds.shape[0], one, (zero, zero))
        sums[0:1, cols] = column_sum(both[0])
        sums[1:2, cols] = column_sum(both[1])


def last_kernel(section, place, number, d1, q0, q1, q2, q3, z1, mi1, gain1, mask, ds, *rest):
    sources, (dz1, keep, give, tot, w, sems) = rest[:7], rest[7:]
    weights = Weights(section, place, sources, w, sems)
    narrow_finish(d1, (q0, q1, q2, q3), z1, mi1, gain1, mask, number, dz1, tot)
    half = keep.shape[0]
    for i, cols in enumerate(blocks(ds.shape[1])):
        weights.wait(i)
        block = lax.dot_general(dz1[...], w[cols, :], last_only, preferred_element_type=f32)
        keep[:, cols] = block[:half] + ds[:half, cols].astype(f32)
        give[:, cols] = (block[half:] + ds[half:, cols].astype(f32)).astype(bf16)


def drop_kernel(codes, cots, head, merged):
    line = lax.broadcasted_iota(jnp.int32, cots.shape[1:], 0)
    bounds = (0, KSEG, KSEG + KDEP, KSEG + KDEP + KNOR)
    cot = cots[0].astype(f32)
    tasks = [
        jnp.where((line >= a) & (line < b), cot, 0.0).T.astype(bf16)
        for a, b in zip(bounds[:-1], bounds[1:])
    ]
    for cols in blocks(head.shape[1], 8):
        g = [jnp.dot(task, head[:, cols], preferred_element_type=f32) for task in tasks]
        total = g[0] + g[1] + g[2]
        magnitude = sum(jnp.sqrt(v * v + DROP_FLOOR * DROP_FLOOR) for v in g)
        purity = 0.5 + 0.5 * (total / magnitude)
        bar = (codes[0, :, cols] + 0.5) / CODE_SCALE
        keep = sigmoid((purity - bar) * DROP_SHARPNESS)
        lose = 1.0 - keep
        value = sum(v * jnp.where(v > 0.0, keep, lose) for v in g)
        merged[:, cols] = value.astype(bf16)


VM = pl.BlockSpec(memory_space=pltpu.VMEM)
SM = pl.BlockSpec(memory_space=pltpu.SMEM)
ANY = pl.BlockSpec(memory_space=pltpu.HBM)


def run(kernel, operands, specs, outs, scratch, flops):
    return pl.pallas_call(
        kernel,
        out_shape=[jax.ShapeDtypeStruct(shape, kind) for shape, kind in outs],
        in_specs=specs,
        out_specs=[VM] * len(outs),
        scratch_shapes=scratch,
        compiler_params=pltpu.CompilerParams(vmem_limit_bytes=LIMIT),
        cost_estimate=pl.CostEstimate(
            flops=flops,
            bytes_accessed=sum(o.size * o.dtype.itemsize for o in operands[:16]),
            transcendentals=0,
        ),
    )(*operands)


def flip(value, bits):
    count = lax.axis_size("dp")
    return lax.ppermute(value, "dp", [(i, i ^ bits) for i in range(count)])


def cross(value, bits):
    count = lax.axis_size("segment")
    return lax.ppermute(value, "segment", [(i, i ^ bits) for i in range(count)])


def turned(value, even, odd):
    size, count = lax.axis_size("segment"), lax.axis_size("dp")
    pairs = [
        (i * count + j, (i ^ (odd if j % 2 else even)) * count + j) for i in range(size) for j in range(count)
    ]
    return lax.ppermute(value, ("segment", "dp"), pairs)


def after(value, *others):
    return lax.optimization_barrier((value,) + others)[0]


def dp_bits():
    count = lax.axis_size("dp")
    return [1 << k for k in range(count.bit_length() - 1)]


def group_bits():
    bits = [b for b in dp_bits() if b != SWAP]
    return bits[:2], bits[2:]


def four_parts(value):
    first, _ = group_bits()
    near = jnp.stack([value, flip(value, first[0])])
    far = flip(near, first[1])
    return [near[0], near[1], far[0], far[1]]


def pair_up(stats, count):
    for b in group_bits()[1]:
        other, other_count = flip(stats, b), flip(count, b)
        whole = count + other_count
        here, there = count[0, 0], other_count[0, 0]
        away = stats[0] / here - other[0] / there
        square = stats[1] + other[1] + away * away * (here * there / (here + there))
        merged = jnp.stack([stats[0] + other[0], square])
        if stats.shape[0] > 2:
            merged = jnp.concatenate([merged, stats[2:] + other[2:]], axis=0)
        stats, count = merged, whole
    return stats


def pair_sum(value):
    for b in group_bits()[1]:
        value = value + flip(value, b)
    return value


def split_rows(value, index, parts=2):
    size = value.shape[0] // parts
    return lax.dynamic_slice_in_dim(value, index * size, size, 0)


def on_device(
    inputs,
    extents,
    wide_weight,
    mid_weight,
    narrow_gain,
    narrow_bias,
    expand_gain,
    expand_bias,
    head_weight,
    head_cotangent,
    drop_codes,
):
    seg = lax.axis_index("segment")
    dp = lax.axis_index("dp")
    sections = lax.axis_size("segment")
    x_side, y_side, core = seg % 2, seg // 2, dp % 2
    swapped = (dp // SWAP) % 2
    channels = inputs.shape[-1]
    narrow = wide_weight.shape[-1]
    half_width = narrow // 2
    classes = head_weight.shape[-1]
    place = jnp.stack([seg, core]).astype(jnp.int32)

    own_small = jnp.concatenate(
        [head_weight.T, jnp.zeros((HEADS - classes, head_weight.shape[0]), bf16), expand_gain.T, expand_bias.T]
        + [narrow_gain, narrow_bias, jnp.zeros((10, narrow), bf16)],
        axis=0,
    )
    small_x = cross(own_small, 1)
    small_y = cross(jnp.stack([own_small, small_x]), 2)
    small = jnp.stack([own_small, small_x, small_y[0], small_y[1]])
    small = jnp.stack([lax.dynamic_index_in_dim(small, k ^ seg, 0, keepdims=False) for k in range(4)])
    lanes = jnp.moveaxis(small[:, : HEADS + 4], 0, 1).reshape(HEADS + 4, channels)
    head_rows = lanes[:HEADS]
    gain_wide = lanes[HEADS : HEADS + 2].astype(f32)
    bias_wide = lanes[HEADS + 2 : HEADS + 4].astype(f32)
    gain_narrow = small[:, HEADS + 4].astype(f32)
    bias_narrow = small[:, HEADS + 5].astype(f32)

    own_count = inputs.shape[0]
    start = seg * own_count

    def own_part(value):
        return lax.dynamic_slice_in_dim(value, start, own_count, 0).astype(f32).reshape(own_count, -1, PIX)

    boxes = jnp.pad(extents, ((0, 0), (0, 0), (0, PIX - 2)))
    facts = jnp.concatenate([own_part(v) for v in (head_cotangent, drop_codes, boxes)], axis=1)
    facts = jnp.pad(facts, ((0, 0), (0, -facts.shape[1] % 8), (0, 0)))
    keep_facts = lax.dynamic_index_in_dim(facts, swapped, 0, keepdims=False)
    got_facts = flip(lax.dynamic_index_in_dim(facts, 1 - swapped, 0, keepdims=False), SWAP)
    facts = jnp.stack([keep_facts, got_facts])
    code_rows = channels // PIX
    cotangent = facts[:, :classes].astype(bf16)
    codes = facts[:, classes : classes + code_rows].reshape(2, 1, channels)
    box = facts[:, classes + code_rows, :2].astype(jnp.int32)
    keep_in = lax.dynamic_index_in_dim(inputs, swapped, 0, keepdims=False)
    give_in = lax.dynamic_index_in_dim(inputs, 1 - swapped, 0, keepdims=False)
    half_pix = PIX // 2
    got_in = [flip(give_in[:, :half_pix], SWAP)]
    got_in.append(flip(after(give_in[:, half_pix:], got_in[0]), SWAP))
    images = 2 * inputs.shape[1]
    rows = images * PIX

    wide_own = wide_weight[0]
    mid_own = mid_weight[0].reshape(-1, narrow)

    def exchange(own, *gate):
        mine = after(split_rows(own, core), *gate)
        return turned(mine, 1, 2), turned(mine, 2, 1)

    def pass_on(own, first, second, *gate):
        pieces = [first, second, turned(after(first, second, *gate), 2, 1)]
        return [own] + pieces + [flip(p, 1) for p in pieces]

    wide = pass_on(wide_own, *exchange(wide_own, give_in), got_in[0], small_x, got_facts)
    mid_two = exchange(mid_own, wide[3])

    local_count = jnp.full((8, 128), jnp.sum(box[:, 0] * box[:, 1]).astype(f32))
    position = jnp.arange(PIX, dtype=jnp.int32)
    inside = (position // FRAME < box[:, 0:1]) & (position % FRAME < box[:, 1:2])
    mask = inside.astype(f32).reshape(rows, 1)

    cot_columns = jnp.pad(cotangent, ((0, 0), (0, HEADS - classes), (0, 0)))
    (merged,) = pl.pallas_call(
        drop_kernel,
        grid=(images,),
        in_specs=[
            pl.BlockSpec((1, 1, channels), lambda i: (i, 0, 0)),
            pl.BlockSpec((1, HEADS, PIX), lambda i: (i, 0, 0)),
            pl.BlockSpec((HEADS, channels), lambda i: (0, 0)),
        ],
        out_specs=[pl.BlockSpec((PIX, channels), lambda i: (i, 0))],
        out_shape=[jax.ShapeDtypeStruct((rows, channels), bf16)],
        compiler_params=pltpu.CompilerParams(vmem_limit_bytes=LIMIT),
    )(codes, cot_columns, head_rows)

    got_in = jnp.concatenate([got_in[0], after(got_in[1], merged)], axis=1)
    entry = jnp.concatenate([keep_in, got_in], axis=0).reshape(rows, channels)

    narrow_f = ((rows, narrow), f32)
    narrow_b = ((rows, narrow), bf16)
    wide_f = ((rows, channels), f32)
    wide_b = ((rows, channels), bf16)
    pair_n = ((2, narrow), f32)
    pair_w = ((2, channels), f32)
    copies_b = ((images, PIX + 2 * PAD, 3 * narrow), bf16)
    w_scratch = [pltpu.VMEM((channels, narrow), bf16), pltpu.SemaphoreType.DMA((4,))]
    m_shape = pltpu.VMEM((9 * half_width, narrow), bf16)
    m_scratch = [m_shape, m_shape, pltpu.SemaphoreType.DMA((4,)), pltpu.SemaphoreType.DMA((4,))]
    w_specs = [ANY] * 7
    product = 2 * rows * channels * narrow
    conv = 2 * rows * 9 * narrow * narrow

    def row(values, k):
        return values[k : k + 1]

    met = {}

    def moments(stats):
        if id(stats) not in met:
            met[id(stats)] = (four_parts(pair_up(stats, local_count)), stats)
        return met[id(stats)][0]

    kept = {}
    z1, st = run(
        functools.partial(first_kernel, 0),
        [place, local_count, entry, mask] + wide,
        [SM, VM, VM, VM] + w_specs,
        [narrow_f, ((8, narrow), f32)],
        w_scratch,
        product,
    )
    mid = pass_on(mid_own, *mid_two, merged, z1)
    group_counts = moments(st)
    number = sum(g[2:3, :128] for g in group_counts)
    group_counts = [g[2:3, :128] for g in group_counts]
    u = entry
    for k in range(2):
        head, tail = 2 * k, 2 * k + 1
        hs, z2, st2, mi1 = run(
            functools.partial(middle_kernel, head),
            [place] + group_counts + [z1] + moments(st) + [row(gain_narrow, head), row(bias_narrow, head), mask] + mid,
            [SM] + [VM] * 12 + w_specs,
            [copies_b, narrow_f, pair_n, pair_n],
            m_scratch,
            conv,
        )
        h2, z3, st3, mi2 = run(
            functools.partial(expand_kernel, tail),
            [place] + group_counts + [z2] + moments(st2) + [row(gain_narrow, tail), row(bias_narrow, tail), mask] + wide,
            [SM] + [VM] * 12 + w_specs,
            [narrow_b, wide_f, pair_w, pair_n],
            w_scratch,
            product,
        )
        kept[k] = dict(z1=z1, mi1=mi1, hs=hs, z2=z2, mi2=mi2, h2=h2, z3=z3, u=u)
        last = [row(gain_wide, k), row(bias_wide, k), u, mask]
        if k == 0:
            u, z1, st, kept[0]["mi3"] = run(
                functools.partial(join_kernel, 2),
                [place] + group_counts + [z3] + moments(st3) + last + wide,
                [SM] + [VM] * 13 + w_specs,
                [wide_b, narrow_f, pair_n, pair_w],
                w_scratch,
                product,
            )
        else:
            ds, n3, sums3, logits, head_grad, mi3 = run(
                turn_kernel,
                group_counts + [z3] + moments(st3) + last + [merged, head_rows, cot_columns],
                [VM] * 16,
                [wide_b, wide_b, pair_w, ((HEADS, rows), f32), ((HEADS, channels), f32), pair_w],
                [pltpu.VMEM((rows, channels // 4), bf16)],
                product // 4,
            )
            kept[1]["mi3"] = mi3

    grads, totals = {}, {}

    def plus(a, b):
        return (a.astype(f32) + b.astype(f32)).astype(bf16)

    def joined(side, mine, other):
        return jnp.where(
            side == 1, jnp.concatenate([other, mine], axis=0), jnp.concatenate([mine, other], axis=0)
        )

    def halves(grad):
        return plus(split_rows(grad, core), flip(split_rows(grad, 1 - core), 1))

    def by_xy(blocks4):
        return [blocks4[i] for i in (0, 2, 1, 3)]

    def quarters(value):
        return jnp.split(value, 4, axis=0)

    z_groups = [[j for j in range(lax.axis_size("dp")) if j % 2 == side] for side in range(2)]

    def slow_xy(blocks4):
        return lax.psum_scatter(jnp.concatenate(by_xy(blocks4), axis=0), "segment", scatter_dimension=0, tiled=True)

    def slow_z(part):
        return lax.psum(part, "dp", axis_index_groups=z_groups)

    first_side, second_side = jnp.where(core == 0, x_side, y_side), jnp.where(core == 0, y_side, x_side)

    def pick(four, start):
        return jnp.stack(
            [lax.dynamic_index_in_dim(four, start + i * (1 + core), 0, keepdims=False) for i in range(2)]
        )

    def quick_sum(blocks4):
        four = jnp.stack(blocks4)
        got = turned(pick(four, (1 - first_side) * (2 - core)), 1, 2)
        yield got
        two = plus(pick(four, first_side * (2 - core)), got)
        got = turned(lax.dynamic_index_in_dim(two, 1 - second_side, 0, keepdims=False), 2, 1)
        yield got
        part = plus(lax.dynamic_index_in_dim(two, second_side, 0, keepdims=False), got)
        bits = dp_bits()[1:]
        for b in bits:
            side = (dp // b) % 2
            part = plus(split_rows(part, side), flip(split_rows(part, 1 - side), b))
        for b in bits[::-1]:
            part = joined((dp // b) % 2, part, flip(part, b))
        return part

    def finish(steps):
        while True:
            try:
                next(steps)
            except StopIteration as end:
                return end.value

    def pair_to_owner(part, k):
        got = lax.ppermute(part, "segment", [(i, i ^ 2) for i in range(sections) if i // 2 != k])
        half = joined(y_side, part, got)
        return joined(core, half, flip(half, 1))

    def tile_grad(left, right, dims=rows_only):
        return lax.dot_general(left, right, dims, preferred_element_type=f32).astype(bf16)

    def conv_grad(hs, dz2, side):
        right = dz2.reshape(images, PIX, narrow)
        both = (((0, 1), (0, 1)), ((), ()))
        width = 3 * half_width
        parts = [
            tile_grad(hs[:, FRAME * d : FRAME * d + PIX, side * width : (side + 1) * width], right, both)
            for d in range(3)
        ]
        return jnp.concatenate(parts, axis=0)

    def sections_of(kind, k):
        pair = [halves(grads[kind, 2 * k + i]) for i in range(2)]
        return [b for v in pair for b in jnp.split(v, 2, axis=0)]

    for k in (1, 0):
        head, tail = 2 * k, 2 * k + 1
        it = kept[k]
        narrow2 = [it["z2"], it["mi2"], row(gain_narrow, tail)]
        narrow1 = [it["z1"], it["mi1"], row(gain_narrow, head)]
        dz3, d2, sums2, totals["wide", k] = run(
            functools.partial(shrink_kernel, tail),
            [place if k else after(place, *four_m1, *four_w1), number, ds, n3] + four_parts(pair_sum(sums3)) + [it["mi3"], row(gain_wide, k), mask]
            + narrow2 + [row(bias_narrow, tail)] + wide,
            [SM] + [VM] * 14 + w_specs,
            [wide_b, narrow_f, pair_n, pair_w],
            w_scratch,
            product,
        )
        grads["w", tail] = tile_grad(dz3, it["h2"])
        hold = place
        if k == 0:
            hold = after(place, w1_step)
            w1_step = next(w1)
        dz2, d1, sums1, totals["narrow", tail] = run(
            functools.partial(unmix_kernel, head),
            [hold, number, d2] + four_parts(pair_sum(sums2)) + narrow2 + [mask] + narrow1
            + [row(bias_narrow, head)] + mid,
            [SM] + [VM] * 14 + w_specs,
            [narrow_b, narrow_f, pair_n, pair_n],
            [pltpu.VMEM(*copies_b)] + m_scratch,
            conv,
        )
        grads["m", head] = conv_grad(it["hs"], dz2, 0)
        grads["m", tail] = conv_grad(it["hs"], dz2, 1)
        if k == 0:
            slow_m1 = slow_xy(four_m1)
            four_m0 = sections_of("m", 0)
            hold = after(place, w1_step, slow_m1, *four_m0)
            slow_m1 = slow_z(slow_m1)
            m0 = quick_sum(four_m0)
        base = [hold, number, d1] + four_parts(pair_sum(sums1)) + narrow1 + [mask, ds]
        if k == 1:
            low = kept[0]
            dz1, ds, n3, sums3, totals["narrow", head] = run(
                functools.partial(widen_kernel, head),
                base + [low["z3"], low["mi3"], row(gain_wide, 0), row(bias_wide, 0), low["u"]] + wide,
                [SM] + [VM] * 16 + w_specs,
                [narrow_b, wide_b, wide_b, pair_w, pair_n],
                [w_scratch[0], pltpu.VMEM((rows, channels // 4), f32), w_scratch[1]],
                product,
            )
            grads["w", head] = tile_grad(it["u"], dz1)
        else:
            dz1, grad_keep, grad_give, totals["narrow", head] = run(
                functools.partial(last_kernel, head),
                base + wide,
                [SM] + [VM] * 11 + w_specs,
                [narrow_b, ((rows // 2, channels), f32), ((rows // 2, channels), bf16), pair_n],
                w_scratch,
                product,
            )
            grads["w", head] = tile_grad(it["u"], dz1)
        if k == 1:
            four_m1 = sections_of("m", 1)
            by_block = head_grad.astype(bf16).reshape(HEADS, 4, narrow).transpose(1, 0, 2)
            extra = halves(by_block.reshape(4, 2, HEADS // 2, narrow).transpose(1, 0, 2, 3).reshape(-1, narrow))
            extra = [quarters(extra)[i] for i in (0, 2, 1, 3)]
            four_w1 = [jnp.concatenate([a, b]) for a, b in zip(sections_of("w", 1), extra)]
            w1 = quick_sum(four_w1)
            w1_step = next(w1)

    w0 = quick_sum(sections_of("w", 0))
    w1, m0, w0 = finish(w1), finish(m0), finish(w0)
    slow_m1 = after(slow_m1, grad_give)
    edge = wide_own.shape[0] // 4
    heads = w1[edge:]
    heads = joined(core, heads, flip(heads, 1))
    mid_grad = jnp.where(y_side == 0, pair_to_owner(m0, 0), pair_to_owner(slow_m1, 1)).astype(f32)
    wide_grad = jnp.where(y_side == 0, pair_to_owner(w0, 0), pair_to_owner(w1[:edge], 1)).astype(f32)

    flat = jnp.concatenate(
        [totals["wide", k].reshape(-1, narrow) for k in range(2)]
        + [totals["narrow", i] for i in range(sections)],
        axis=0,
    )
    flat = flat + flip(flat, SWAP)
    flat = flat + cross(flat, 1)
    flat = flat + cross(flat, 2)
    wide_count = 4 * channels // narrow
    wide_all = flat[:wide_count].reshape(2, 2, channels)
    narrow_all = lax.dynamic_index_in_dim(
        flat[wide_count:].reshape(sections, 2, narrow), seg, 0, keepdims=False
    )
    share = channels // sections
    wide_mine = lax.dynamic_slice_in_dim(wide_all, seg * share, share, 2)

    head_out = heads[:classes].astype(f32).T

    def returned(keep, give):
        got = flip(give, SWAP).astype(f32)
        return jnp.stack([jnp.where(swapped == 0, keep, got), jnp.where(swapped == 0, got, keep)])

    by_image = logits[:classes].reshape(classes, images, PIX).transpose(1, 0, 2)
    logits_out = returned(by_image[: images // 2], by_image[images // 2 :].astype(bf16))
    shape = (images // 2, PIX, channels)
    input_grad = returned(grad_keep.reshape(shape), grad_give.reshape(shape))

    return (
        logits_out,
        input_grad,
        wide_grad[None],
        mid_grad.reshape(1, 9, half_width, narrow),
        narrow_all[1:2],
        narrow_all[0:1],
        wide_mine[:, 1].T,
        wide_mine[:, 0].T,
        head_out,
    )


def solution(mesh):
    return jax.shard_map(
        on_device,
        mesh=mesh,
        in_specs=(
            P("segment", "dp", None, None),
            P(None, "dp", None),
            P("segment", None, None),
            P("segment", None, None, None),
            P("segment", None),
            P("segment", None),
            P("segment", None),
            P("segment", None),
            P("segment", None),
            P(None, "dp", None, None),
            P(None, "dp", None),
        ),
        out_specs=(
            P("segment", "dp", None, None),
            P("segment", "dp", None, None),
            P("segment", None, None),
            P("segment", None, None, None),
            P("segment", None),
            P("segment", None),
            P("segment", None),
            P("segment", None),
            P("segment", None),
        ),
        check_vma=False,
    )
```

time: 773 us -> 504 us (0.65)
  starting transfers between devices: 213 us -> 96.9 us
  Pallas kernels: 0 us -> 91.4 us
  waiting for transfers between devices: 227 us -> 166 us
  other arithmetic: 97.9 us -> 51.8 us
  matrix products: 60.4 us -> 14.3 us
  blocking collectives: 46 us -> 0 us
  local copies, waits for them, and re-layouts: 97.7 us -> 57.9 us
    ppermute x82 -> x20, starting transfers between devices: 150 us -> 43.5 us  [the longest x12 19.6 us: turned(): return lax.ppermute(value, ('segment', 'dp'), pairs)]
    pallas_call x0 -> x14, Pallas kernels: none -> 91.4 us  [the longest x13 81.1 us: run(): pl.pallas_call(kernel, out_shape=[jax.ShapeDtypeStruct(shape, kind) for s...]
    dot_general x28 -> x16, matrix products: 60.4 us -> 14.3 us  [tile_grad(): lax.dot_general(left, right, dims, preferred_element_type=f32).astype(bf16)]
    all_gather x2 -> x0, blocking collectives: 46 us -> none  [the longest x1 38.8 us: on_device(): lax.all_gather(jnp.concatenate([narrow_gain, narrow_bias], axis=0), 'segm...]
    ppermute x72 -> x62, waiting for transfers between devices: 115 us -> 75.6 us  [flip(): return lax.ppermute(value, 'dp', [(i, i ^ bits) for i in range(count)])]
    slice x38 -> x10, local copies, waits for them, and re-layouts: 28.2 us -> 4.28 us  [the longest x1 1.56 us: on_device(): by_image[images // 2:].astype(bf16)]
    ppermute x82 -> x20, waiting for transfers between devices: 90.5 us -> 71.1 us  [the longest x12 53.1 us: turned(): return lax.ppermute(value, ('segment', 'dp'), pairs)]
    rsqrt x6 -> x0, other arithmetic: 16.1 us -> none  [group_moments(): return (mean, lax.rsqrt(square / whole + EPS))]
  transfers between devices with their start and end apart: 156 -> 84, of which waited for: 44 -> 38; matrix products, arithmetic and copies ran while one was open for 28% -> 17% of each run, Pallas kernels for 0% -> 10%
where the time goes in v2:
time: 504 us; the launch traced here: 495 us
  waiting for transfers between devices  166 us (33%)
  starting transfers between devices  96.9 us (19%)
  Pallas kernels  91.4 us (18%)
  local copies, waits for them, and re-layouts  57.9 us (11%)
  other arithmetic  51.8 us (10%)
  between operations  17.2 us (3%)
  matrix products  14.3 us (3%)
    pallas_call x13, Pallas kernels, run(): pl.pallas_call(kernel, out_shape=[jax.ShapeDtypeStruct(shape, kind) for s...  81.1 us
    ppermute x62, waiting for transfers between devices, flip(): return lax.ppermute(value, 'dp', [(i, i ^ bits) for i in range(count)])  75.6 us
    ppermute x62, starting transfers between devices, flip(): return lax.ppermute(value, 'dp', [(i, i ^ bits) for i in range(count)])  53.3 us
    ppermute x12, waiting for transfers between devices, turned(): return lax.ppermute(value, ('segment', 'dp'), pairs)  53.1 us
    unnamed x243, local copies, waits for them, and re-layouts  34.1 us
    ppermute x12, starting transfers between devices, turned(): return lax.ppermute(value, ('segment', 'dp'), pairs)  19.6 us
    psum x1, waiting for transfers between devices, slow_z(): return lax.psum(part, 'dp', axis_index_groups=z_groups)  18.8 us
    convert_element_type x21, other arithmetic, plus(): return (a.astype(f32) + b.astype(f32)).astype(bf16)  15.7 us
  transfers between devices with their start and end apart: 84, of which 38 were waited for; matrix products, arithmetic and copies ran while one was open for 17% of the time, Pallas kernels for 10%

profile of v2, /device:TPU:0, one launch (start us, length us, event | category | flops | bytes accessed | tf_op | source)
XLA Modules:
  0.0 495.0 jit_solution(16841190768158201456)
XLA Ops:
  22.9 8.1 %collective-permute-done = f32[56,256]{1,0:T(8,128)S(1)} collective-permute-done((f32[56,256]{1,0:T(8,128)S(1)}, f32[56,256]{1,0:T(8,128)S(1)}, u32[]{:S(2)}, u32[]{:S(2)}) %collective-permute-start) | collective-permute-done | bytes 57376 | tf_op jit(solution)/shard_map/ppermute | solution.py:445
  30.9 8.4 %collective-permute-done.3 = bf16[80,512]{1,0:T(8,128)(2,1)S(1)} collective-permute-done((bf16[80,512]{1,0:T(8,128)(2,1)S(1)}, bf16[80,512]{1,0:T(8,128)(2,1)S(1)}, u32[]{:S(2)}, u32[]{:S(2)}) %collective-permute-start.3) | collective-permute-done | bytes 81952 | tf_op jit(solution)/shard_map/ppermute | solution.py:450
  46.6 9.5 %collective-permute-done.7.rest_3_ = bf16[1024,512]{1,0:T(8,128)(2,1)} collective-permute-done((bf16[1024,512]{1,0:T(8,128)(2,1)S(1)}, bf16[1024,512]{1,0:T(8,128)(2,1)}, u32[]{:S(2)}, u32[]{:S(2)}) %collective-permute-start.7) | collective-permute-done | bytes 1048608 | tf_op jit(solution)/shard_map/ppermute | solution.py:458
  61.4 10.3 %shard_map.178.merged = bf16[512,2048]{1,0:T(8,128)(2,1)S(1)} custom-call(f32[2,1,2048]{2,1,0:T(1,128)S(1)} %reshape.474.codes, bf16[2,64,256]{2,1,0:T(8,128)(2,1)S(1)} %pad.14.cots.cot, bf16[64,2048]{1,0:T(8,128)(2,1)S(1)} %bitcast.289), custom_call_target="tpu_custom_call" | custom-call | tf_op jit(solution)/shard_map/pallas_call | solution.py:591
  77.1 5.8 %collective-permute-done.13.rest_1_ = bf16[1152,512]{1,0:T(8,128)(2,1)S(1)} collective-permute-done((bf16[1152,512]{1,0:T(8,128)(2,1)}, bf16[1152,512]{1,0:T(8,128)(2,1)S(1)}, u32[]{:S(2)}, u32[]{:S(2)}) %collective-permute-start.13) | collective-permute-done | bytes 1179680 | tf_op jit(solution)/shard_map/ppermute | solution.py:458
  85.1 14.1 %collective-permute-done.15.rest_3_ = bf16[1152,512]{1,0:T(8,128)(2,1)S(1)} collective-permute-done((bf16[1152,512]{1,0:T(8,128)(2,1)S(1)}, bf16[1152,512]{1,0:T(8,128)(2,1)S(1)}, u32[]{:S(2)}, u32[]{:S(2)}) %collective-permute-start.15) | collective-permute-done | bytes 1179680 | tf_op jit(solution)/shard_map/ppermute | solution.py:458
  107.7 6.7 %shard_map.180 = (bf16[2,288,1536]{2,1,0:T(8,128)(2,1)S(1)}, f32[512,512]{1,0:T(8,128)S(1)}, f32[2,512]{1,0:T(2,128)S(1)}, f32[2,512]{1,0:T(2,128)S(1)}) custom-call(s32[2]{0:T(128)S(1)} %pad_add_fusion.place, f32[1,128]{1,0:T(1,128)S(1)} %get-tuple-element.202.k0, f32[1,128]{1,0:T(1,128)S(1)} %get-tuple-element.203.k1, f32[1,128]{1,0:T(1,128)S(1)} %get-tuple-element.204.k2, ...), custom_call_target="tpu_custom_call" | custom-call | flops 2415919104 | bytes 5840904 | tf_op jit(solution)/shard_map/pallas_call | solution.py:428
  121.5 8.9 %shard_map.181 = (bf16[512,512]{1,0:T(8,128)(2,1)S(1)}, f32[512,2048]{1,0:T(8,128)S(1)}, f32[2,2048]{1,0:T(2,128)S(1)}, f32[2,512]{1,0:T(2,128)S(1)}) custom-call(s32[2]{0:T(128)S(1)} %pad_add_fusion.place, f32[1,128]{1,0:T(1,128)S(1)} %get-tuple-element.202.k0, f32[1,128]{1,0:T(1,128)S(1)} %get-tuple-element.203.k1, f32[1,128]{1,0:T(1,128)S(1)} %get-tuple-element.204.k2, ...), custom_call_target="tpu_custom_call" | custom-call | flops 1073741824 | bytes 5267464 | tf_op jit(solution)/shard_map/pallas_call | solution.py:428
  136.6 6.4 %shard_map.182 = (bf16[512,2048]{1,0:T(8,128)(2,1)S(1)}, f32[512,512]{1,0:T(8,128)S(1)}, f32[2,512]{1,0:T(2,128)S(1)}, f32[2,2048]{1,0:T(2,128)S(1)}) custom-call(s32[2]{0:T(128)S(1)} %pad_add_fusion.place, f32[1,128]{1,0:T(1,128)S(1)} %get-tuple-element.202.k0, f32[1,128]{1,0:T(1,128)S(1)} %get-tuple-element.203.k1, f32[1,128]{1,0:T(1,128)S(1)} %get-tuple-element.204.k2, ...), custom_call_target="tpu_custom_call" | custom-call | flops 1073741824 | bytes 9523208 | tf_op jit(solution)/shard_map/pallas_call | solution.py:428
  148.9 6.5 %shard_map.183 = (bf16[2,288,1536]{2,1,0:T(8,128)(2,1)S(1)}, f32[512,512]{1,0:T(8,128)S(1)}, f32[2,512]{1,0:T(2,128)S(1)}, f32[2,512]{1,0:T(2,128)S(1)}) custom-call(s32[2]{0:T(128)S(1)} %pad_add_fusion.place, f32[1,128]{1,0:T(1,128)S(1)} %get-tuple-element.202.k0, f32[1,128]{1,0:T(1,128)S(1)} %get-tuple-element.203.k1, f32[1,128]{1,0:T(1,128)S(1)} %get-tuple-element.204.k2, ...), custom_call_target="tpu_custom_call" | custom-call | flops 2415919104 | bytes 5791752 | tf_op jit(solution)/shard_map/pallas_call | solution.py:428
  162.4 9.3 %shard_map.184 = (bf16[512,512]{1,0:T(8,128)(2,1)S(1)}, f32[512,2048]{1,0:T(8,128)S(1)}, f32[2,2048]{1,0:T(2,128)S(1)}, f32[2,512]{1,0:T(2,128)S(1)}) custom-call(s32[2]{0:T(128)S(1)} %pad_add_fusion.place, f32[1,128]{1,0:T(1,128)S(1)} %get-tuple-element.202.k0, f32[1,128]{1,0:T(1,128)S(1)} %get-tuple-element.203.k1, f32[1,128]{1,0:T(1,128)S(1)} %get-tuple-element.204.k2, ...), custom_call_target="tpu_custom_call" | custom-call | flops 1073741824 | bytes 5267464 | tf_op jit(solution)/shard_map/pallas_call | solution.py:428
  178.6 5.3 %shard_map.185 = (bf16[512,2048]{1,0:T(8,128)(2,1)S(1)}, bf16[512,2048]{1,0:T(8,128)(2,1)S(1)}, f32[2,2048]{1,0:T(2,128)S(1)}, f32[64,512]{1,0:T(8,128)S(1)}, f3...) custom-call(f32[1,128]{1,0:T(1,128)S(1)} %get-tuple-element.202.k0, f32[1,128]{1,0:T(1,128)S(1)} %get-tuple-element.203.k1, ...), custom_call_target="tpu_custom_call" | custom-call | flops 268435456 | bytes 8802304 | tf_op jit(solution)/shard_map/pallas_call | solution.py:428
  213.1 5.8 %shard_map.186 = (bf16[512,2048]{1,0:T(8,128)(2,1)S(1)}, f32[512,512]{1,0:T(8,128)S(1)}, f32[2,512]{1,0:T(2,128)S(1)}, f32[2,2048]{1,0:T(2,128)S(1)}) custom-call(s32[2]{0:T(128)S(1)} %pad_add_fusion.place, f32[1,128]{1,0:T(1,128)S(1)} %get-tuple-element.201.number, bf16[512,2048]{1,0:T(8,128)(2,1)S(1)} %copy-done.53, bf16[512,2048]{1,0:T(8,128)(2,1)S(1)} %copy-done.62, ...), custom_call_target="tpu_custom_call" | custom-call | flops 1073741824 | bytes 7440904 | tf_op jit(solution)/shard_map/pallas_call | solution.py:428
  221.1 3.9 collective-permute-done.33
  225.1 6.0 %shard_map.187 = (bf16[512,512]{1,0:T(8,128)(2,1)S(1)}, f32[512,512]{1,0:T(8,128)S(1)}, f32[2,512]{1,0:T(2,128)S(1)}, f32[2,512]{1,0:T(2,128)S(1)}) custom-call(s32[2]{0:T(128)S(1)} %pad_add_fusion.place, f32[1,128]{1,0:T(1,128)S(1)} %get-tuple-element.201.number, f32[512,512]{1,0:T(8,128)S(1)} %get-tuple-element.97.d2, f32[2,512]{1,0:T(2,128)S(1)} %get-tuple-element.98.q0, ...), custom_call_target="tpu_custom_call" | custom-call | flops 2415919104 | bytes 5538312 | tf_op jit(solution)/shard_map/pallas_call | solution.py:428
  236.3 4.2 collective-permute-done.35
  240.6 7.5 %shard_map.188 = (bf16[512,512]{1,0:T(8,128)(2,1)S(1)}, bf16[512,2048]{1,0:T(8,128)(2,1)S(1)}, bf16[512,2048]{1,0:T(8,128)(2,1)S(1)}, f32[2,2048]{1,0:T(2,128)S(1)}, f32[2,512]{1,0:T(2,128)S(1)}) custom-call(s32[2]{0:T(128)S(1)} %pad_add_fusion.place, f32[1,128]{1,0:T(1,128)S(1)} %get-tuple-element.201.number, f32[512,512]{1,0:T(8,128)S(1)} %get-tuple-element.100.d1, ...), custom_call_target="tpu_custom_call" | custom-call | flops 1073741824 | bytes 8446472 | tf_op jit(solution)/shard_map/pallas_call | solution.py:428
  250.0 4.7 collective-permute-done.44
  265.2 5.8 %shard_map.189 = (bf16[512,2048]{1,0:T(8,128)(2,1)S(1)}, f32[512,512]{1,0:T(8,128)S(1)}, f32[2,512]{1,0:T(2,128)S(1)}, f32[2,2048]{1,0:T(2,128)S(1)}) custom-call(s32[2]{0:T(128)S(1)} %pad_add_fusion.place, f32[1,128]{1,0:T(1,128)S(1)} %get-tuple-element.201.number, bf16[512,2048]{1,0:T(8,128)(2,1)S(1)} %get-tuple-element.112.ds, ...), custom_call_target="tpu_custom_call" | custom-call | flops 1073741824 | bytes 7440904 | tf_op jit(solution)/shard_map/pallas_call | solution.py:428
  285.5 5.8 %shard_map.190 = (bf16[512,512]{1,0:T(8,128)(2,1)S(1)}, f32[512,512]{1,0:T(8,128)S(1)}, f32[2,512]{1,0:T(2,128)S(1)}, f32[2,512]{1,0:T(2,128)S(1)}) custom-call(s32[2]{0:T(128)S(1)} %pad_add_fusion.place, f32[1,128]{1,0:T(1,128)S(1)} %get-tuple-element.201.number, f32[512,512]{1,0:T(8,128)S(1)} %copy-done.64, f32[2,512]{1,0:T(2,128)S(1)} %get-tuple-element.117.q0, ...), custom_call_target="tpu_custom_call" | custom-call | flops 2415919104 | bytes 5538312 | tf_op jit(solution)/shard_map/pallas_call | solution.py:428
  299.0 4.5 collective-permute-done.50
  308.8 11.8 %collective-permute-done.40 = bf16[544,512]{1,0:T(8,128)(2,1)} collective-permute-done((bf16[544,512]{1,0:T(8,128)(2,1)S(1)}, bf16[544,512]{1,0:T(8,128)(2,1)}, u32[]{:S(2)}, u32[]{:S(2)}) %collective-permute-start.40) | collective-permute-done | bytes 557088 | tf_op jit(solution)/shard_map/ppermute | solution.py:458
  350.6 11.0 %collective-permute-done.69 = bf16[576,512]{1,0:T(8,128)(2,1)} collective-permute-done((bf16[576,512]{1,0:T(8,128)(2,1)S(1)}, bf16[576,512]{1,0:T(8,128)(2,1)}, u32[]{:S(2)}, u32[]{:S(2)}) %collective-permute-start.69) | collective-permute-done | bytes 589856 | tf_op jit(solution)/shard_map/ppermute | solution.py:458
  369.9 4.0 collective-permute-start.71
  382.7 9.5 %collective-permute-done.56 = bf16[256,512]{1,0:T(8,128)(2,1)S(1)} collective-permute-done((bf16[256,512]{1,0:T(8,128)(2,1)S(1)}, bf16[256,512]{1,0:T(8,128)(2,1)S(1)}, u32[]{:S(2)}, u32[]{:S(2)}) %collective-permute-start.56) | collective-permute-done | bytes 262176 | tf_op jit(solution)/shard_map/ppermute | solution.py:445
  393.0 3.8 collective-permute-done.65
  406.0 7.9 %collective-permute-done.78 = f32[24,512]{1,0:T(8,128)S(1)} collective-permute-done((f32[24,512]{1,0:T(8,128)S(1)}, f32[24,512]{1,0:T(8,128)S(1)}, u32[]{:S(2)}, u32[]{:S(2)}) %collective-permute-start.78) | collective-permute-done | bytes 49184 | tf_op jit(solution)/shard_map/ppermute | solution.py:445
  413.9 8.1 %collective-permute-start.79 = (f32[24,512]{1,0:T(8,128)S(1)}, f32[24,512]{1,0:T(8,128)S(1)}, u32[]{:S(2)}, u32[]{:S(2)}) collective-permute-start(f32[24,512]{1,0:T(8,128)S(1)} %add.353), channel_id=1, source_target_pairs={{0,8},{8,0},{16,24},{24,16},{1,9},{9,1},{17,25},{25,17},{2,10},{10... | collective-permute-start | bytes 147464 | tf_op jit(solution)/shard_map/ppermute | solution.py:450
  430.9 18.8 %all-reduce.5.cloned.1.call-done = bf16[576,512]{1,0:T(8,128)(2,1)} async-done(((bf16[576,512]{1,0:T(8,128)(2,1)}), bf16[576,512]{1,0:T(8,128)(2,1)}) %all-reduce.5.cloned.1.call-update) | async-done | bytes 589840 | tf_op jit(solution)/shard_map/psum | solution.py:710
  449.7 4.2 collective-permute-start.76
  468.2 7.0 %collective-permute-done.60 = bf16[512,512]{1,0:T(8,128)(2,1)S(1)} collective-permute-done((bf16[512,512]{1,0:T(8,128)(2,1)S(1)}, bf16[512,512]{1,0:T(8,128)(2,1)S(1)}, u32[]{:S(2)}, u32[]{:S(2)}) %collective-permute-start.60) | collective-permute-done | bytes 524320 | tf_op jit(solution)/shard_map/ppermute | solution.py:743
  484.3 3.7 fusion.4
  (576 shorter events, 240.5 us)
Async XLA Ops:
  7.2 313.5 %reduce-scatter.2.cloned.1.call-start = ((), (), s32[]{:S(2)}) async-start(), calls=%async_computation.1 | async-start | bytes 2949120 | tf_op jit(solution)/shard_map/reduce_scatter | solution.py:707
  11.0 28.4 %collective-permute-start.5 = (bf16[1024,512]{1,0:T(8,128)(2,1)}, bf16[1024,512]{1,0:T(8,128)(2,1)S(1)}, u32[]{:S(2)}, u32[]{:S(2)}) collective-permute-start(bf16[1024,512]{1,0:T(8,128)(2,1)} %dynamic-slice_bitcast_fusion), channel_id=1, source_target_pairs={{0,8},{1,17},{2,10},{3,19},{4,12},{5,21},{6,14},{7,23},{8,0},{9,25... | collective-permute-start | bytes 3145736 | tf_op jit(solution)/shard_map/ppermute | solution.py:458
  14.0 25.4 %collective-permute-start.6 = (bf16[1024,512]{1,0:T(8,128)(2,1)}, bf16[1024,512]{1,0:T(8,128)(2,1)}, u32[]{:S(2)}, u32[]{:S(2)}) collective-permute-start(bf16[1024,512]{1,0:T(8,128)(2,1)} %dynamic-slice_bitcast_fusion), channel_id=1, source_target_pairs={{0,16},{1,9},{2,18},{3,11},{4,20},{5,13},{6,22},{7,15},{8,24},{9,1... | collective-permute-start | bytes 3145736 | tf_op jit(solution)/shard_map/ppermute | solution.py:458
  16.4 23.0 %collective-permute-start.1 = (bf16[1,128,2048]{2,1,0:T(8,128)(2,1)}, bf16[1,128,2048]{2,1,0:T(8,128)(2,1)S(1)}, u32[]{:S(2)}, u32[]{:S(2)}) collective-permute-start(bf16[1,128,2048]{2,1,0:T(8,128)(2,1)} %get-tuple-element.169), channel_id=1, source_target_pairs={{0,2},{1,3},{2,0},{3,1},{4,6},{5,7},{6,4},{7,5},{8,10},{9,11},{10,... | collective-permute-start | bytes 1572872 | tf_op jit(solution)/shard_map/ppermute | solution.py:445
  19.9 19.5 %collective-permute-start.3 = (bf16[80,512]{1,0:T(8,128)(2,1)S(1)}, bf16[80,512]{1,0:T(8,128)(2,1)S(1)}, u32[]{:S(2)}, u32[]{:S(2)}) collective-permute-start(bf16[80,512]{1,0:T(8,128)(2,1)S(1)} %concatenate.205), channel_id=1, source_target_pairs={{0,8},{8,0},{16,24},{24,16},{1,9},{9,1},{17,25},{25,17},{2,10},{10... | collective-permute-start | bytes 245768 | tf_op jit(solution)/shard_map/ppermute | solution.py:450
  41.3 19.8 %collective-permute-start.2 = (bf16[1,128,2048]{2,1,0:T(8,128)(2,1)S(1)}, bf16[1,128,2048]{2,1,0:T(8,128)(2,1)}, u32[]{:S(2)}, u32[]{:S(2)}) collective-permute-start(bf16[1,128,2048]{2,1,0:T(8,128)(2,1)S(1)} %get-tuple-element.72), channel_id=1, source_target_pairs={{0,2},{1,3},{2,0},{3,1},{4,6},{5,7},{6,4},{7,5},{8,10},{9,11},{10,... | collective-permute-start | bytes 1572872 | tf_op jit(solution)/shard_map/ppermute | solution.py:445
  46.1 27.1 %collective-permute-start.8 = (bf16[1024,512]{1,0:T(8,128)(2,1)S(1)}, bf16[1024,512]{1,0:T(8,128)(2,1)S(1)}, u32[]{:S(2)}, u32[]{:S(2)}) collective-permute-start(bf16[1024,512]{1,0:T(8,128)(2,1)S(1)} %collective-permute-done.5.rest_1_), channel_id=1, source_target_pairs={{0,1},{1,0},{2,3},{3,2},{4,5},{5,4},{6,7},{7,6},{8,9},{9,8},{10,11... | collective-permute-start | bytes 3145736 | tf_op jit(solution)/shard_map/ppermute | solution.py:445
  46.1 27.1 %collective-permute-start.9 = (bf16[1024,512]{1,0:T(8,128)(2,1)}, bf16[1024,512]{1,0:T(8,128)(2,1)S(1)}, u32[]{:S(2)}, u32[]{:S(2)}) collective-permute-start(bf16[1024,512]{1,0:T(8,128)(2,1)} %collective-permute-done.6.rest_2_), channel_id=1, source_target_pairs={{0,1},{1,0},{2,3},{3,2},{4,5},{5,4},{6,7},{7,6},{8,9},{9,8},{10,11... | collective-permute-start | bytes 3145736 | tf_op jit(solution)/shard_map/ppermute | solution.py:445
  56.1 26.8 %collective-permute-start.13 = (bf16[1152,512]{1,0:T(8,128)(2,1)}, bf16[1152,512]{1,0:T(8,128)(2,1)S(1)}, u32[]{:S(2)}, u32[]{:S(2)}) collective-permute-start(bf16[1152,512]{1,0:T(8,128)(2,1)} %constant_dynamic-slice_fusion.31), channel_id=1, source_target_pairs={{0,8},{1,17},{2,10},{3,19},{4,12},{5,21},{6,14},{7,23},{8,0},{9,25... | collective-permute-start | bytes 3538952 | tf_op jit(solution)/shard_map/ppermute | solution.py:458
  58.7 24.4 %collective-permute-start.14 = (bf16[1152,512]{1,0:T(8,128)(2,1)}, bf16[1152,512]{1,0:T(8,128)(2,1)S(1)}, u32[]{:S(2)}, u32[]{:S(2)}) collective-permute-start(bf16[1152,512]{1,0:T(8,128)(2,1)} %constant_dynamic-slice_fusion.31), channel_id=1, source_target_pairs={{0,16},{1,9},{2,18},{3,11},{4,20},{5,13},{6,22},{7,15},{8,24},{9,1... | collective-permute-start | bytes 3538952 | tf_op jit(solution)/shard_map/ppermute | solution.py:458
  84.6 23.0 %collective-permute-start.16 = (bf16[1152,512]{1,0:T(8,128)(2,1)S(1)}, bf16[1152,512]{1,0:T(8,128)(2,1)S(1)}, u32[]{:S(2)}, u32[]{:S(2)}) collective-permute-start(bf16[1152,512]{1,0:T(8,128)(2,1)S(1)} %collective-permute-done.13.rest_1_), channel_id=1, source_target_pairs={{0,1},{1,0},{2,3},{3,2},{4,5},{5,4},{6,7},{7,6},{8,9},{9,8},{10,11... | collective-permute-start | bytes 3538952 | tf_op jit(solution)/shard_map/ppermute | solution.py:445
  84.6 23.0 %collective-permute-start.17 = (bf16[1152,512]{1,0:T(8,128)(2,1)S(1)}, bf16[1152,512]{1,0:T(8,128)(2,1)S(1)}, u32[]{:S(2)}, u32[]{:S(2)}) collective-permute-start(bf16[1152,512]{1,0:T(8,128)(2,1)S(1)} %collective-permute-done.14.rest_2_), channel_id=1, source_target_pairs={{0,1},{1,0},{2,3},{3,2},{4,5},{5,4},{6,7},{7,6},{8,9},{9,8},{10,11... | collective-permute-start | bytes 3538952 | tf_op jit(solution)/shard_map/ppermute | solution.py:445
  197.5 57.1 %collective-permute-start.37 = (bf16[128,512]{1,0:T(8,128)(2,1)}, bf16[128,512]{1,0:T(8,128)(2,1)}, u32[]{:S(2)}, u32[]{:S(2)}) collective-permute-start(bf16[128,512]{1,0:T(8,128)(2,1)} %constant_dynamic-slice_fusion.29), channel_id=1, source_target_pairs={{0,1},{1,0},{2,3},{3,2},{4,5},{5,4},{6,7},{7,6},{8,9},{9,8},{10,11... | collective-permute-start | bytes 393224 | tf_op jit(solution)/shard_map/ppermute | solution.py:445
  202.4 143.8 %collective-permute-start.29 = (bf16[1,44,256]{2,0,1:T(2,128)(2,1)}, bf16[1,44,256]{2,0,1:T(2,128)(2,1)}, u32[]{:S(2)}, u32[]{:S(2)}) collective-permute-start(bf16[1,44,256]{2,0,1:T(2,128)(2,1)} %slice.533), channel_id=1, source_target_pairs={{0,2},{1,3},{2,0},{3,1},{4,6},{5,7},{6,4},{7,5},{8,10},{9,11},{10,... | collective-permute-start | bytes 67592 | tf_op jit(solution)/shard_map/ppermute | solution.py:445
  220.8 35.3 %collective-permute-start.38 = (bf16[1024,512]{1,0:T(8,128)(2,1)S(1)}, bf16[1024,512]{1,0:T(8,128)(2,1)}, u32[]{:S(2)}, u32[]{:S(2)}) collective-permute-start(bf16[1024,512]{1,0:T(8,128)(2,1)S(1)} %constant_dynamic-slice_fusion.28), channel_id=1, source_target_pairs={{0,1},{1,0},{2,3},{3,2},{4,5},{5,4},{6,7},{7,6},{8,9},{9,8},{10,11... | collective-permute-start | bytes 3145736 | tf_op jit(solution)/shard_map/ppermute | solution.py:445
  235.1 28.4 %collective-permute-start.41 = (bf16[1152,512]{1,0:T(8,128)(2,1)S(1)}, bf16[1152,512]{1,0:T(8,128)(2,1)S(1)}, u32[]{:S(2)}, u32[]{:S(2)}) collective-permute-start(bf16[1152,512]{1,0:T(8,128)(2,1)S(1)} %constant_dynamic-slice_fusion.23), channel_id=1, source_target_pairs={{0,1},{1,0},{2,3},{3,2},{4,5},{5,4},{6,7},{7,6},{8,9},{9,8},{10,11... | collective-permute-start | bytes 3538952 | tf_op jit(solution)/shard_map/ppermute | solution.py:445
  262.0 20.8 %collective-permute-start.39 = (bf16[2,544,512]{2,1,0:T(8,128)(2,1)}, bf16[2,544,512]{2,1,0:T(8,128)(2,1)}, u32[]{:S(2)}, u32[]{:S(2)}) collective-permute-start(bf16[2,544,512]{2,1,0:T(8,128)(2,1)} %pad_maximum_fusion.10), channel_id=1, source_target_pairs={{0,8},{1,17},{2,10},{3,19},{4,12},{5,21},{6,14},{7,23},{8,0},{9,25... | collective-permute-start | bytes 3342344 | tf_op jit(solution)/shard_map/ppermute | solution.py:458
  274.9 174.8 %all-reduce.5.cloned.1.call-start = ((), (), s32[]{:S(2)}) async-start(), calls=%async_computation.2 | async-start | bytes 1179648 | tf_op jit(solution)/shard_map/psum | solution.py:710
  279.4 54.5 %collective-permute-start.53 = (bf16[1024,512]{1,0:T(8,128)(2,1)}, bf16[1024,512]{1,0:T(8,128)(2,1)}, u32[]{:S(2)}, u32[]{:S(2)}) collective-permute-start(bf16[1024,512]{1,0:T(8,128)(2,1)} %constant_dynamic-slice_fusion.18), channel_id=1, source_target_pairs={{0,1},{1,0},{2,3},{3,2},{4,5},{5,4},{6,7},{7,6},{8,9},{9,8},{10,11... | collective-permute-start | bytes 3145736 | tf_op jit(solution)/shard_map/ppermute | solution.py:445
  307.3 32.4 %collective-permute-start.68 = (bf16[2,576,512]{2,1,0:T(8,128)(2,1)}, bf16[2,576,512]{2,1,0:T(8,128)(2,1)}, u32[]{:S(2)}, u32[]{:S(2)}) collective-permute-start(bf16[2,576,512]{2,1,0:T(8,128)(2,1)} %pad_maximum_fusion.9), channel_id=1, source_target_pairs={{0,8},{1,17},{2,10},{3,19},{4,12},{5,21},{6,14},{7,23},{8,0},{9,25... | collective-permute-start | bytes 3538952 | tf_op jit(solution)/shard_map/ppermute | solution.py:458
  344.1 19.5 %collective-permute-start.54 = (bf16[2,512,512]{2,1,0:T(8,128)(2,1)}, bf16[2,512,512]{2,1,0:T(8,128)(2,1)}, u32[]{:S(2)}, u32[]{:S(2)}) collective-permute-start(bf16[2,512,512]{2,1,0:T(8,128)(2,1)} %pad_maximum_fusion.11), channel_id=1, source_target_pairs={{0,8},{1,17},{2,10},{3,19},{4,12},{5,21},{6,14},{7,23},{8,0},{9,25... | collective-permute-start | bytes 3145736 | tf_op jit(solution)/shard_map/ppermute | solution.py:458
  348.2 18.6 %collective-permute-start.63 = (bf16[136,512]{1,0:T(8,128)(2,1)S(1)}, bf16[136,512]{1,0:T(8,128)(2,1)S(1)}, u32[]{:S(2)}, u32[]{:S(2)}) collective-permute-start(bf16[136,512]{1,0:T(8,128)(2,1)S(1)} %constant_dynamic-slice_fusion.10), channel_id=1, source_target_pairs={{0,4},{1,5},{2,6},{3,7},{4,0},{5,1},{6,2},{7,3},{8,12},{9,13},{10,... | collective-permute-start | bytes 417800 | tf_op jit(solution)/shard_map/ppermute | solution.py:445
  382.1 18.0 %collective-permute-start.72 = (bf16[144,512]{1,0:T(8,128)(2,1)S(1)}, bf16[144,512]{1,0:T(8,128)(2,1)S(1)}, u32[]{:S(2)}, u32[]{:S(2)}) collective-permute-start(bf16[144,512]{1,0:T(8,128)(2,1)S(1)} %add_convert_fusion.14), channel_id=1, source_target_pairs={{0,4},{1,5},{2,6},{3,7},{4,0},{5,1},{6,2},{7,3},{8,12},{9,13},{10,... | collective-permute-start | bytes 442376 | tf_op jit(solution)/shard_map/ppermute | solution.py:445
  397.0 52.7 %collective-permute-start.66 = (bf16[512,512]{1,0:T(8,128)(2,1)S(1)}, bf16[512,512]{1,0:T(8,128)(2,1)}, u32[]{:S(2)}, u32[]{:S(2)}) collective-permute-start(bf16[512,512]{1,0:T(8,128)(2,1)S(1)} %slice.444), channel_id=1, source_target_pairs={{0,16},{8,24},{1,17},{9,25},{2,18},{10,26},{3,19},{11,27},{4,20},{... | collective-permute-start | bytes 1572872 | tf_op jit(solution)/shard_map/ppermute | solution.py:743
  400.1 21.9 %collective-permute-start.73 = (bf16[288,512]{1,0:T(8,128)(2,1)S(1)}, bf16[288,512]{1,0:T(8,128)(2,1)}, u32[]{:S(2)}, u32[]{:S(2)}) collective-permute-start(bf16[288,512]{1,0:T(8,128)(2,1)S(1)} %maximum_select_fusion.11), channel_id=1, source_target_pairs={{0,2},{1,3},{2,0},{3,1},{4,6},{5,7},{6,4},{7,5},{8,10},{9,11},{10,... | collective-permute-start | bytes 884744 | tf_op jit(solution)/shard_map/ppermute | solution.py:445
  403.3 21.3 %collective-permute-start.58 = (bf16[128,512]{1,0:T(8,128)(2,1)S(1)}, bf16[128,512]{1,0:T(8,128)(2,1)S(1)}, u32[]{:S(2)}, u32[]{:S(2)}) collective-permute-start(bf16[128,512]{1,0:T(8,128)(2,1)S(1)} %add_convert_fusion.16), channel_id=1, source_target_pairs={{0,4},{1,5},{2,6},{3,7},{4,0},{5,1},{6,2},{7,3},{8,12},{9,13},{10,... | collective-permute-start | bytes 393224 | tf_op jit(solution)/shard_map/ppermute | solution.py:445
  406.0 18.7 %collective-permute-start.81 = (bf16[32,512]{1,0:T(8,128)(2,1)S(1)}, bf16[32,512]{1,0:T(8,128)(2,1)S(1)}, u32[]{:S(2)}, u32[]{:S(2)}) collective-permute-start(bf16[32,512]{1,0:T(8,128)(2,1)S(1)} %slice.447), channel_id=1, source_target_pairs={{0,1},{1,0},{2,3},{3,2},{4,5},{5,4},{6,7},{7,6},{8,9},{9,8},{10,11... | collective-permute-start | bytes 98312 | tf_op jit(solution)/shard_map/ppermute | solution.py:445
  423.3 37.4 %collective-permute-start.74 = (bf16[576,512]{1,0:T(8,128)(2,1)S(1)}, bf16[576,512]{1,0:T(8,128)(2,1)}, u32[]{:S(2)}, u32[]{:S(2)}) collective-permute-start(bf16[576,512]{1,0:T(8,128)(2,1)S(1)} %maximum_select_fusion.8), channel_id=1, source_target_pairs={{16,0},{24,8},{17,1},{25,9},{18,2},{26,10},{19,3},{27,11},{20,4},{... | collective-permute-start | bytes 1769480 | tf_op jit(solution)/shard_map/ppermute | solution.py:743
  424.6 33.1 %collective-permute-start.59 = (bf16[256,512]{1,0:T(8,128)(2,1)S(1)}, bf16[256,512]{1,0:T(8,128)(2,1)}, u32[]{:S(2)}, u32[]{:S(2)}) collective-permute-start(bf16[256,512]{1,0:T(8,128)(2,1)S(1)} %maximum_select_fusion.13), channel_id=1, source_target_pairs={{0,2},{1,3},{2,0},{3,1},{4,6},{5,7},{6,4},{7,5},{8,10},{9,11},{10,... | collective-permute-start | bytes 786440 | tf_op jit(solution)/shard_map/ppermute | solution.py:445
  425.4 50.3 %collective-permute-start.51 = (bf16[1,256,2048]{2,1,0:T(8,128)(2,1)S(1)}, bf16[1,256,2048]{2,1,0:T(8,128)(2,1)}, u32[]{:S(2)}, u32[]{:S(2)}) collective-permute-start(bf16[1,256,2048]{2,1,0:T(8,128)(2,1)S(1)} %bitcast.323), channel_id=1, source_target_pairs={{0,2},{1,3},{2,0},{3,1},{4,6},{5,7},{6,4},{7,5},{8,10},{9,11},{10,... | collective-permute-start | bytes 3145736 | tf_op jit(solution)/shard_map/ppermute | solution.py:445
  427.4 28.1 %collective-permute-start.80 = (f32[24,512]{1,0:T(8,128)S(1)}, f32[24,512]{1,0:T(8,128)}, u32[]{:S(2)}, u32[]{:S(2)}) collective-permute-start(f32[24,512]{1,0:T(8,128)S(1)} %add.354), channel_id=1, source_target_pairs={{0,16},{8,24},{16,0},{24,8},{1,17},{9,25},{17,1},{25,9},{2,18},{10... | collective-permute-start | bytes 147464 | tf_op jit(solution)/shard_map/ppermute | solution.py:450
  455.5 28.8 %collective-permute-start.67 = (bf16[1024,512]{1,0:T(8,128)(2,1)S(1)}, bf16[1024,512]{1,0:T(8,128)(2,1)}, u32[]{:S(2)}, u32[]{:S(2)}) collective-permute-start(bf16[1024,512]{1,0:T(8,128)(2,1)S(1)} %maximum_select_fusion.7), channel_id=1, source_target_pairs={{0,1},{1,0},{2,3},{3,2},{4,5},{5,4},{6,7},{7,6},{8,9},{9,8},{10,11... | collective-permute-start | bytes 3145736 | tf_op jit(solution)/shard_map/ppermute | solution.py:445
  (170 other events, 1909.6 us)
Sparse Core Ops, SparseCore 0:
  275.0 37.8 reduce-scatter.1
  402.5 47.1 all-reduce.4
